TPU v7x, 256 devices: a whole 4x4x8 slice. The times are simulated.
256 devices in a mesh: gx: 8 (over y, z_lo), gy: 32 (over z_hi, x, core).
Axes of the slice: x: 4, y: 4, z: 8 (z_hi: 4, z_lo: 2; z = z_hi * 2 + z_lo), core: 2. Of those that a mesh axis runs over, the one named last changes fastest.
Arguments:
- density: float32 [8, 4096, 8192], P(None, 'gx', 'gy'), may hold values from -6 to 6
Outputs:
- refactored: float32 [8, 4096, 8192], P(None, 'gx', 'gy')
All inputs are finite; a program needn't handle non-finite values.
Results may differ from a plain program's by a relative error of at most 0.000096.
Values sent between devices are 32-bit elements; how exact they have to be, the bound alone decides.
No kernel may reach another device: no remote copies, remote signals or barrier semaphores. Data moves between devices by JAX's collectives and lax.ppermute only.
A program may use at most 128 MiB of HBM per device.

v0:
```python
import functools

import jax
import jax.numpy as jnp
import numpy as np
from jax import lax
from jax.experimental import pallas as pl
from jax.experimental.pallas import tpu as pltpu
from jax.sharding import PartitionSpec as P

ROOT = np.sqrt(3.0) - 2.0
CENTRE = 3.0 / np.sqrt(12.0)
F32 = jnp.float32


def line_operators(fine):
    n = fine // 2
    load = np.zeros((3 * n, 3 * fine))
    even = np.zeros((3 * n, 3 * n))
    for j in range(3 * n):
        for at, weight in ((2 * j, 1 / 3), (2 * j - 2, -1 / 6), (2 * j + 2, -1 / 6),
                           (2 * j - 1, 0.5), (2 * j + 1, 0.5)):
            if 0 <= at < 3 * fine:
                load[j, at] = weight
        for at, weight in ((j, 5 / 6), (j - 1, 1 / 12), (j + 1, 1 / 12)):
            if 0 <= at < 3 * n:
                even[j, at] = weight
    place = np.arange(3 * n)
    solve = CENTRE * ROOT ** np.abs(place[:, None] - place[None, :])
    a = (solve @ load)[:, fine:2 * fine]
    d = (solve @ even)[:, n:2 * n]
    near = np.arange(n)
    return dict(
        n=n, a=a[n:2 * n], a_left=a[n - 1], a_right=a[2 * n],
        d=d[n:2 * n], d_left=d[n - 1], d_right=d[2 * n],
        from_left=ROOT ** near, from_right=ROOT ** (n - 1 - near),
    )


def on_even(rows):
    wide = np.zeros(rows.shape[:-1] + (2 * rows.shape[-1],))
    wide[..., ::2] = rows
    return wide


def two_levels(fine):
    one = line_operators(fine)
    two = line_operators(one["n"])
    functionals = dict(
        a_left=two["a_left"], a_right=two["a_right"],
        d_left=on_even(two["d_left"]), d_right=on_even(two["d_right"]),
    )
    return one, two, functionals


def x_tables(fine):
    one, two, f = two_levels(fine)
    n = one["n"]
    rows = n + 8
    own = []
    for kind in ("a", "d"):
        table = np.zeros((rows, one[kind].shape[1]))
        left, right = one[kind + "_left"], one[kind + "_right"]
        table[:n] = one[kind]
        table[n] = right
        table[n + 1] = (f["a_right"] @ one["from_right"]) * left
        table[n + 2] = (f["a_left"] @ one["from_left"]) * right
        table[n + 3] = (f["d_right"] @ one["from_right"]) * left
        table[n + 4] = (f["d_left"] @ one["from_left"]) * right
        own.append(table)
    send = []
    for side in ("left", "right"):
        parts = []
        for kind in ("a", "d", "e"):
            part = np.zeros((16, fine))
            if kind == "e":
                part[8], part[9] = on_even(f["a_" + side]), on_even(f["d_" + side])
            else:
                base, step = (0, 1) if kind == "a" else (4, 2)
                part[base, ::step] = one[kind + "_" + side]
                part[base + 1, ::step] = f["a_" + side] @ one[kind]
                part[base + 2, ::step] = f["d_" + side] @ one[kind]
                part[base + 3, ::step] = one[kind][0]
            parts.append(part)
        send.append(parts)
    receive = np.zeros((rows, 32))
    for base in (0, 4):
        receive[:n, base] = one["from_left"]
        receive[n + 1, base + 1] = 1
        receive[n + 3, base + 2] = 1
        receive[:n, 16 + base] = one["from_right"]
        receive[n + 2, 16 + base + 1] = 1
        receive[n + 4, 16 + base + 2] = 1
        receive[n, 16 + base + 3] = 1
    receive[n + 1, 8] = receive[n + 3, 9] = 1
    receive[n + 2, 16 + 8] = receive[n + 4, 16 + 9] = receive[n, 16 + 10] = 1
    m = n // 2
    level2_a, level2_d = np.zeros((m, rows)), np.zeros((m, rows))
    level2_a[:, :n], level2_d[:, :n] = two["a"], on_even(two["d"])
    level2_a[:, n + 1], level2_a[:, n + 2] = two["from_left"], two["from_right"]
    level2_d[:, n + 3], level2_d[:, n + 4] = two["from_left"], two["from_right"]
    return own, send, receive, np.concatenate([level2_a, level2_d], 0)


def y_tables(fine):
    one, two, f = two_levels(fine)
    n = one["n"]
    kinds = []
    for kind in ("e", "a", "d"):
        table = np.zeros((fine, 2 * n))
        if kind == "e":
            inside = on_even(np.eye(n))
            left = right = np.zeros(fine)
        else:
            widen = on_even if kind == "d" else (lambda rows: rows)
            inside = widen(one[kind])
            left, right = widen(one[kind + "_left"]), widen(one[kind + "_right"])
        table[:, :n] = inside.T
        table[:, n] = right
        table[:, n + 1] = (f["a_right"] @ one["from_right"]) * left
        table[:, n + 2] = (f["a_left"] @ one["from_left"]) * right
        table[:, n + 3] = (f["d_right"] @ one["from_right"]) * left
        table[:, n + 4] = (f["d_left"] @ one["from_left"]) * right
        table[:, n + 8], table[:, n + 9] = left, right
        for at, name in enumerate(("a_left", "a_right", "d_left", "d_right")):
            table[:, n + 10 + at] = f[name] @ inside
        table[:, n + 14] = inside[0]
        kinds.append(-table if kind == "d" else table)
    receive = np.zeros((16, 2 * n))
    receive[1, :n] = one["from_left"]
    receive[3, n + 1] = receive[5, n + 3] = 1
    receive[8, :n] = one["from_right"]
    receive[10, n + 2] = receive[12, n + 4] = receive[14, n] = 1
    m = n // 2
    level2 = np.zeros((3, 2 * n, m))
    level2[0, :n] = on_even(np.eye(m)).T
    level2[1, :n] = two["a"].T
    level2[1, n + 1], level2[1, n + 2] = two["from_left"], two["from_right"]
    level2[2, :n] = -on_even(two["d"]).T
    level2[2, n + 3], level2[2, n + 4] = -two["from_left"], -two["from_right"]
    spread2 = on_even(level2).reshape(6 * n, n)
    return np.concatenate(kinds, 0), receive, spread2, on_even(np.eye(n))


def z_tables(planes):
    n = planes // 2
    predict, spread = np.eye(planes), np.zeros((planes, n))
    mass, restrict, solve = (np.zeros(s) for s in ((planes, planes), (n, planes), (n, n)))
    for i in range(planes):
        for at, weight in ((i, 4 / 6), (i - 1, 1 / 6), (i + 1, 1 / 6)):
            mass[i, at % planes] += weight
        if i % 2:
            predict[i, i - 1] -= 0.5
            predict[i, (i + 1) % planes] -= 0.5
    for j in range(n):
        spread[2 * j, j] = 1
        for at, weight in ((2 * j, 1.0), (2 * j - 1, 0.5), (2 * j + 1, 0.5)):
            restrict[j, at % planes] += weight
        for at, weight in ((j, 4 / 3), (j - 1, 1 / 3), (j + 1, 1 / 3)):
            solve[j, at % n] += weight
    load = np.linalg.inv(solve) @ restrict @ mass
    return (load @ predict).tolist(), (load @ spread).tolist()


def dot(a, b, dims=((1,), (0,))):
    return lax.dot_general(
        a, b, (dims, ((), ())), precision=lax.Precision.HIGHEST, preferred_element_type=F32
    )


def combine(weights, planes):
    total = None
    for weight, plane in zip(weights, planes):
        term = plane * float(weight)
        total = term if total is None else total + term
    return total


def parity_of(axis):
    return (lax.axis_index(axis) % 2).astype(jnp.int32).reshape(1)


def swap(first, second, axis):
    size = lax.axis_size(axis)
    inner = [(i, i ^ 1) for i in range(size)]
    outer = [(i, (i + 1) % size if i % 2 else (i - 1) % size) for i in range(size)]
    return lax.ppermute(first, axis, inner), lax.ppermute(second, axis, outer)


def edge_kernel(z_a, z_d, parity, top, bottom, left_table, right_table, first, second):
    planes = top.shape[0]

    def message(strip, table, row):
        fine = [strip[k] for k in range(planes)]
        even = fine[::2]
        a = [combine(weights, fine) for weights in z_a]
        d = [combine(weights, even) for weights in z_d]
        cat = [jnp.concatenate([a[k], d[k], even[k]], 0) for k in range(planes // 2)]
        out = dot(table[...], jnp.concatenate(cat, 1))
        if row:
            index = lax.broadcasted_iota(jnp.int32, out.shape, 0)
            firsts = jnp.concatenate([strip[k, :1, :] for k in range(0, planes, 2)], 1)
            others = jnp.concatenate([strip[k, :1, :] for k in range(1, planes, 2)], 1)
            out = jnp.where(index == 10, firsts, jnp.where(index == 11, others, out))
        return out

    to_left = message(top, left_table, True)
    to_right = message(bottom, right_table, False)
    odd = parity[0] == 1
    first[...] = jnp.where(odd, to_left, to_right)
    second[...] = jnp.where(odd, to_right, to_left)


def own_kernel(z_a, z_d, low, high, a_table, d_table, y_table, c, column):
    planes, fine, lanes = low.shape
    n, width = fine // 2, 2 * lanes
    halves = (low, high)
    whole = [jnp.concatenate([part[k] for part in halves], 1) for k in range(planes)]
    even = [
        jnp.concatenate([part[k, pl.ds(0, n, stride=2), :] for part in halves], 1)
        for k in range(0, planes, 2)
    ]
    for z in range(planes // 2):
        x_a = dot(a_table[...], combine(z_a[z], whole))
        x_d = dot(d_table[...], combine(z_d[z], even))
        total = dot(x_a, y_table[width:2 * width]) + dot(x_d, y_table[2 * width:])
        c[z] = total
        c[z, :n] = total[:n] + dot(even[z], y_table[:width])
    for k in range(planes):
        column[k:k + 1, :] = low[k].T[:1, :]


def join_kernel(parity, c_own, column, first, second, receive, y_table, c, message):
    half, rows, width = c_own.shape
    odd = parity[0] == 1
    from_left = jnp.where(odd, first[...], second[...])
    from_right = jnp.where(odd, second[...], first[...])
    both = jnp.concatenate([from_left, from_right], 0)
    stacked = jnp.concatenate(
        [both[:, z * width:(z + 1) * width] for z in range(half)], 0
    )
    kind = lax.broadcasted_iota(jnp.int32, stacked.shape, 0) % 16
    typed = jnp.concatenate(
        [
            jnp.where(kind >= 8, stacked, 0.0),
            jnp.where(kind < 4, stacked, 0.0),
            jnp.where((kind >= 4) & (kind < 8), stacked, 0.0),
        ],
        1,
    )
    processed = dot(typed, y_table[...])
    lanes = message.shape[1]
    message[...] = jnp.zeros_like(message)
    for z in range(half):
        field = c_own[z] + dot(receive[...], processed[32 * z:32 * z + 32])
        c[z] = field
        side = field[:, width // 2:].T
        message[:, z * 384:z * 384 + rows] = side[8:16]
    u0 = column[...]
    fine = u0.shape[1]
    plane = lax.broadcasted_iota(jnp.int32, u0.shape, 0)
    lane = lax.broadcasted_iota(jnp.int32, u0.shape, 1)
    after = pltpu.roll(u0, fine - 1, 1)
    for z in range(half):
        for k, row in ((2 * z, 10), (2 * z + 1, 11)):
            corner = from_right[row:row + 1, z * width:z * width + 1]
            after = jnp.where((plane == k) & (lane == fine - 1), corner, after)
    before = pltpu.roll(u0, 1, 1)
    u0 = jnp.where(lane % 2 == 1, u0 - 0.5 * (before + after), u0)
    around = pltpu.roll(u0, 1, 0) + pltpu.roll(u0, 2 * half - 1, 0)
    message[:, lanes - fine:] = jnp.where(plane % 2 == 1, u0 - 0.5 * around, u0)


def detail_kernel(parity, u, first, second, w):
    planes, fine, width = u.shape
    odd = parity[0] == 1
    from_right = jnp.where(odd, second[...], first[...])
    row = lax.broadcasted_iota(jnp.int32, (fine, width), 0)
    lane = lax.broadcasted_iota(jnp.int32, (fine, width), 1)

    def along_x(k):
        plane = u[k]
        at = (k // 2) * width
        halo = from_right[10 + k % 2:11 + k % 2, at:at + width]
        after = jnp.where(row == fine - 1, halo, pltpu.roll(plane, fine - 1, 0))
        before = pltpu.roll(plane, 1, 0)
        return jnp.where(row % 2 == 1, plane - 0.5 * (before + after), plane)

    def along_y(plane):
        after = jnp.where(lane == width - 1, 0.0, pltpu.roll(plane, width - 1, 1))
        before = pltpu.roll(plane, 1, 1)
        return jnp.where(lane % 2 == 1, plane - 0.5 * (before + after), plane)

    start = along_x(0)
    even = start
    for k in range(0, planes, 2):
        w[k] = along_y(even)
        following = start if k + 2 == planes else along_x(k + 2)
        w[k + 1] = along_y(along_x(k + 1) - 0.5 * (even + following))
        even = following


def last_kernel(z_a, z_d, parity, c, w, first, second, receive, x_table, y_table, spread, out, inner):
    half, rows, width = c.shape
    planes, fine, lanes = out.shape
    n, m = fine // 2, width // 2
    at = pl.program_id(0)
    odd = parity[0] == 1
    from_right = jnp.where(odd, second[...], first[...])

    @pl.when(at == 0)
    def _():
        from_left = jnp.where(odd, first[...], second[...])
        both = jnp.concatenate([from_left, from_right], 0)
        coarse = []
        for z in range(half):
            sides = both[:, z * 384:(z + 1) * 384].T[:rows]
            coarse.append(c[z] + dot(sides, receive[...]))

        def along_xy(field):
            after = pltpu.roll(field, rows - 1, 0)
            before = pltpu.roll(field, 1, 0)
            index = lax.broadcasted_iota(jnp.int32, field.shape, 0)
            field = jnp.where(index % 2 == 1, field - 0.5 * (before + after), field)[:n]
            after = pltpu.roll(field, width - 1, 1)
            before = pltpu.roll(field, 1, 1)
            index = lax.broadcasted_iota(jnp.int32, field.shape, 1)
            return jnp.where(index % 2 == 1, field - 0.5 * (before + after), field)[:, :m]

        details = [along_xy(field) for field in coarse]
        for z in range(0, half, 2):
            inner[z] = details[z]
            around = details[z] + details[(z + 2) % half]
            inner[z + 1] = details[z + 1] - 0.5 * around
        level = [dot(x_table[...], field) for field in coarse]
        quarter = n // 2
        level_a = [part[:quarter] for part in level]
        level_d = [part[quarter:] for part in level[::2]]
        mark = lax.broadcasted_iota(jnp.int32, (quarter, m), 1) % 2 == 0
        for z in range(half // 2):
            a = combine(z_a[z], level_a)
            d = combine(z_d[z], level_d)
            here = pl.ds(0, quarter, stride=2)
            values = dot(a, y_table[width:2 * width]) + dot(d, y_table[2 * width:])
            old = inner[2 * z, here, :]
            inner[2 * z, here, :] = jnp.where(mark, old + values, old)

    column = from_right[:, from_right.shape[1] - fine:].T
    lane = lax.broadcasted_iota(jnp.int32, (fine, lanes), 1)
    last = (lane == lanes - 1) & (at == pl.num_programs(0) - 1)
    for k in range(planes):
        out[k] = jnp.where(last, w[k] - 0.5 * column[:, k:k + 1], w[k])
    even_lane = lax.broadcasted_iota(jnp.int32, (n, lanes), 1) % 2 == 0
    for z in range(half):
        wide = dot(inner[z], spread[...])
        here = (2 * z, pl.ds(0, n, stride=2), slice(None))
        out[here] = jnp.where(even_lane, wide, out[here])


def shards(density):
    planes, fine, width = density.shape
    half, n = planes // 2, fine // 2
    depth = min(64, fine)
    z_a, z_d = z_tables(planes)
    z2_a, z2_d = z_tables(half)
    (own_a, own_d), send, x_receive, x_level2 = x_tables(fine)
    y_table, y_receive, y_level2, y_spread = y_tables(width)
    rows = n + 8
    left = np.concatenate([part[:, :depth] for part in send[0]], 1)
    right = np.concatenate([part[:, fine - depth:] for part in send[1]], 1)
    as32 = lambda table: jnp.asarray(table, F32)
    params = pltpu.CompilerParams(vmem_limit_bytes=48 * 2**20)
    smem = pl.BlockSpec(memory_space=pltpu.SMEM)
    vmem = pl.BlockSpec(memory_space=pltpu.VMEM)
    shape = lambda *dims: jax.ShapeDtypeStruct(dims, F32)
    parity_x, parity_y = parity_of("gx"), parity_of("gy")

    to_inner, to_outer = pl.pallas_call(
        functools.partial(edge_kernel, z_a, z_d),
        out_shape=(shape(16, half * width),) * 2,
        grid=(1,),
        in_specs=[
            smem,
            pl.BlockSpec((planes, depth, width), lambda i: (0, 0, 0)),
            pl.BlockSpec((planes, depth, width), lambda i: (0, fine // depth - 1, 0)),
            vmem, vmem,
        ],
        out_specs=[vmem, vmem],
        compiler_params=params,
        name="edges",
    )(parity_x, density, density, as32(left), as32(right))
    inner_x, outer_x = swap(to_inner, to_outer, "gx")

    c_own, column = pl.pallas_call(
        functools.partial(own_kernel, z_a, z_d),
        out_shape=(shape(half, rows, width), shape(planes, fine)),
        grid=(1,),
        in_specs=[
            pl.BlockSpec((planes, fine, width // 2), lambda i: (0, 0, 0)),
            pl.BlockSpec((planes, fine, width // 2), lambda i: (0, 0, 1)),
        ] + [vmem] * 3,
        out_specs=[vmem] * 2,
        compiler_params=params,
        name="own",
    )(density, density, as32(own_a), as32(own_d), as32(y_table))

    c, message = pl.pallas_call(
        join_kernel,
        out_shape=(shape(half, rows, width), shape(8, half * 384 + fine)),
        in_specs=[smem] + [vmem] * 6,
        out_specs=[vmem] * 2,
        compiler_params=params,
        name="join",
    )(parity_x, c_own, column, inner_x, outer_x, as32(x_receive), as32(y_table))
    inner_y, outer_y = swap(message, message, "gy")

    w = pl.pallas_call(
        detail_kernel,
        out_shape=shape(planes, fine, width),
        in_specs=[smem] + [vmem] * 3,
        out_specs=vmem,
        compiler_params=params,
        name="details",
    )(parity_x, density, inner_x, outer_x)

    return pl.pallas_call(
        functools.partial(last_kernel, z2_a, z2_d),
        out_shape=shape(planes, fine, width),
        grid=(width // 128,),
        in_specs=[
            smem,
            vmem,
            pl.BlockSpec((planes, fine, 128), lambda i: (0, 0, i)),
            vmem, vmem, vmem, vmem, vmem,
            pl.BlockSpec((width // 2, 128), lambda i: (0, i)),
        ],
        out_specs=pl.BlockSpec((planes, fine, 128), lambda i: (0, 0, i)),
        scratch_shapes=[pltpu.VMEM((half, n, width // 2), F32)],
        compiler_params=params,
        name="last",
    )(parity_y, c, w, inner_y, outer_y, as32(y_receive), as32(x_level2), as32(y_level2), as32(y_spread))


def solution(mesh):
    spec = P(None, "gx", "gy")
    return jax.shard_map(shards, mesh=mesh, in_specs=(spec,), out_specs=spec, check_vma=False)
```

profile of v0, /device:TPU:1, one launch (start us, length us, event | category | flops | bytes accessed | tf_op | source)
XLA Modules:
  0.0 45.4 jit_solution(14018811219462244481)
XLA Ops:
  0.0 0.0 copy-start
  0.0 2.2 %copy-done = f32[8,512,256]{2,1,0:T(8,128)S(1)} copy-done((f32[8,512,256]{2,1,0:T(8,128)S(1)}, f32[8,512,256]{2,1,0:T(8,128)}, u32[]{:S(2)}) %copy-start) | copy-done | bytes 4194328
  2.2 0.0 copy-start.10
  2.2 0.7 %copy-done.10 = f32[16,192]{1,0:T(8,128)S(1)} copy-done((f32[16,192]{1,0:T(8,128)S(1)}, f32[16,192]{1,0:T(8,128)}, u32[]{:S(2)}) %copy-start.10) | copy-done | bytes 12312
  2.9 0.0 copy-start.11
  2.9 0.7 %copy-done.11 = f32[16,192]{1,0:T(8,128)S(1)} copy-done((f32[16,192]{1,0:T(8,128)S(1)}, f32[16,192]{1,0:T(8,128)}, u32[]{:S(2)}) %copy-start.11) | copy-done | bytes 12312
  3.6 0.0 copy-start.2
  3.6 0.0 copy-start.3
  3.6 0.0 copy-start.6
  3.6 1.1 %edges.1 = (f32[16,1024]{1,0:T(8,128)S(1)}, f32[16,1024]{1,0:T(8,128)S(1)}) custom-call(s32[1]{0:T(128)} %bitcast.1.parity, f32[8,512,256]{2,1,0:T(8,128)S(1)} %copy-done, f32[8,512,256]{2,1,0:T(8,128)S(1)} %copy-done, f32[16,192]{1,0:T(8,128)S(1)} %copy-done.11, f32[16,192]{1,0:T(8,128)S(1)} %copy-done.10), custom_call_target="tpu_custom_call" | custom-call | tf_op jit(solution)/shard_map/edges/pallas_call | solution.py:378
  4.7 2.5 %collective-permute-start = (f32[16,1024]{1,0:T(8,128)S(1)}, f32[16,1024]{1,0:T(8,128)S(1)}, u32[]{:S(2)}, u32[]{:S(2)}) collective-permute-start(f32[16,1024]{1,0:T(8,128)S(1)} %get-tuple-element.13), channel_id=1, source_target_pairs={{0,32},{32,0},{64,96},{96,64},{128,160},{160,128},{192,224},{224,1... | collective-permute-start | bytes 196616 | tf_op jit(solution)/shard_map/ppermute | solution.py:187
  7.2 0.0 copy-start.7
  7.2 2.5 %collective-permute-start.1 = (f32[16,1024]{1,0:T(8,128)S(1)}, f32[16,1024]{1,0:T(8,128)S(1)}, u32[]{:S(2)}, u32[]{:S(2)}) collective-permute-start(f32[16,1024]{1,0:T(8,128)S(1)} %get-tuple-element.14), channel_id=1, source_target_pairs={{0,224},{32,64},{64,32},{96,128},{128,96},{160,192},{192,160},{224... | collective-permute-start | bytes 196616 | tf_op jit(solution)/shard_map/ppermute | solution.py:187
  9.7 0.0 copy-done.2
  9.7 0.0 copy-done.3
  9.7 0.0 copy-done.6
  9.7 9.4 %own.1 = (f32[4,264,256]{2,1,0:T(8,128)S(1)}, f32[8,512]{1,0:T(8,128)S(1)}) custom-call(f32[8,512,256]{2,1,0:T(8,128)} %u.1, f32[8,512,256]{2,1,0:T(8,128)} %u.1, f32[264,512]{1,0:T(8,128)S(1)} %copy-done.3, f32[264,256]{1,0:T(8,128)S(1)} %copy-done.6, f32[768,256]{1,0:T(8,128)S(1)} %copy-done.2), custom_call_target="tpu_custom_call" | custom-call | tf_op jit(solution)/shard_map/own/pallas_call | solution.py:394
  19.1 0.0 collective-permute-done.first
  19.1 0.0 collective-permute-done.1.second
  19.1 0.0 copy-done.7
  19.2 2.1 %join.1 = (f32[4,264,256]{2,1,0:T(8,128)S(1)}, f32[8,2048]{1,0:T(8,128)S(1)}) custom-call(s32[1]{0:T(128)} %bitcast.1.parity, f32[4,264,256]{2,1,0:T(8,128)S(1)} %get-tuple-element.11.c_own, f32[8,512]{1,0:T(8,128)S(1)} %get-tuple-element.12.column, f32[16,1024]{1,0:T(8,128)S(1)} %collective-permute-done.first, ...), custom_call_target="tpu_custom_call" | custom-call | tf_op jit(solution)/shard_map/join/pallas_call | solution.py:407
  21.2 2.2 %collective-permute-start.3 = (f32[8,2048]{1,0:T(8,128)S(1)}, f32[8,2048]{1,0:T(8,128)S(1)}, u32[]{:S(2)}, u32[]{:S(2)}) collective-permute-start(f32[8,2048]{1,0:T(8,128)S(1)} %get-tuple-element.16), channel_id=1, source_target_pairs={{0,31},{1,2},{2,1},{3,4},{4,3},{5,6},{6,5},{7,8},{8,7},{9,10},{10,... | collective-permute-start | bytes 196616 | tf_op jit(solution)/shard_map/ppermute | solution.py:187
  23.4 6.3 %collective-permute-start.2 = (f32[8,2048]{1,0:T(8,128)S(1)}, f32[8,2048]{1,0:T(8,128)S(1)}, u32[]{:S(2)}, u32[]{:S(2)}) collective-permute-start(f32[8,2048]{1,0:T(8,128)S(1)} %get-tuple-element.16), channel_id=1, source_target_pairs={{0,1},{1,0},{2,3},{3,2},{4,5},{5,4},{6,7},{7,6},{8,9},{9,8},{10,11... | collective-permute-start | bytes 196616 | tf_op jit(solution)/shard_map/ppermute | solution.py:187
  29.7 0.0 copy-start.4
  29.7 0.0 copy-start.5
  29.7 0.0 copy-start.8
  29.7 0.0 copy-start.9
  29.7 5.7 %details.1.w = f32[8,512,256]{2,1,0:T(8,128)S(1)} custom-call(s32[1]{0:T(128)} %bitcast.1.parity, f32[8,512,256]{2,1,0:T(8,128)} %u.1, f32[16,1024]{1,0:T(8,128)S(1)} %collective-permute-done.first, f32[16,1024]{1,0:T(8,128)S(1)} %collective-permute-done.1.second), custom_call_target="tpu_custom_call" | custom-call | tf_op jit(solution)/shard_map/details/pallas_call | solution.py:417
  35.3 0.0 copy-start.1
  35.3 1.9 %copy-done.1 = f32[8,512,256]{2,1,0:T(8,128)} copy-done((f32[8,512,256]{2,1,0:T(8,128)}, f32[8,512,256]{2,1,0:T(8,128)S(1)}, u32[]{:S(2)}) %copy-start.1) | copy-done | bytes 4194328
  37.3 0.0 collective-permute-done.3.second
  37.3 0.0 collective-permute-done.2.first
  37.3 0.0 copy-done.4
  37.3 0.0 copy-done.5
  37.3 0.0 copy-done.8
  37.3 0.0 copy-done.9
  37.3 8.1 %last.1 = f32[8,512,256]{2,1,0:T(8,128)} custom-call(s32[1]{0:T(128)} %bitcast.parity, f32[4,264,256]{2,1,0:T(8,128)S(1)} %get-tuple-element.15.c, f32[8,512,256]{2,1,0:T(8,128)} %copy-done.1, f32[8,2048]{1,0:T(8,128)S(1)} %collective-permute-done.2.first, f32[8,2048]{1,0:T(8,128)S(1)} %collective-permute-done.3.second, f32[16,256]{1,0:T(8,128)S(1)} %copy-done.9, ...), custom_call_target="tpu_custom_call" | custom-call | tf_op jit(solution)/shard_map/last/pallas_call | solution.py:426
Async XLA Ops:
  0.0 2.2 %copy-start = (f32[8,512,256]{2,1,0:T(8,128)S(1)}, f32[8,512,256]{2,1,0:T(8,128)}, u32[]{:S(2)}) copy-start(f32[8,512,256]{2,1,0:T(8,128)} %u.1) | copy-start | bytes 12582916
  2.2 0.7 %copy-start.10 = (f32[16,192]{1,0:T(8,128)S(1)}, f32[16,192]{1,0:T(8,128)}, u32[]{:S(2)}) copy-start(f32[16,192]{1,0:T(8,128)} %constant.47.clone.right_table) | copy-start | bytes 36868
  2.9 0.7 %copy-start.11 = (f32[16,192]{1,0:T(8,128)S(1)}, f32[16,192]{1,0:T(8,128)}, u32[]{:S(2)}) copy-start(f32[16,192]{1,0:T(8,128)} %constant.46.clone.left_table) | copy-start | bytes 36868
  3.6 6.1 %copy-start.2 = (f32[768,256]{1,0:T(8,128)S(1)}, f32[768,256]{1,0:T(8,128)}, u32[]{:S(2)}) copy-start(f32[768,256]{1,0:T(8,128)} %constant.50.clone.y_table) | copy-start | bytes 2359300
  3.6 6.1 %copy-start.3 = (f32[264,512]{1,0:T(8,128)S(1)}, f32[264,512]{1,0:T(8,128)}, u32[]{:S(2)}) copy-start(f32[264,512]{1,0:T(8,128)} %constant.48.clone.a_table) | copy-start | bytes 1622020
  3.6 6.1 %copy-start.6 = (f32[264,256]{1,0:T(8,128)S(1)}, f32[264,256]{1,0:T(8,128)}, u32[]{:S(2)}) copy-start(f32[264,256]{1,0:T(8,128)} %constant.49.clone.d_table) | copy-start | bytes 811012
  4.7 14.4 %collective-permute-start = (f32[16,1024]{1,0:T(8,128)S(1)}, f32[16,1024]{1,0:T(8,128)S(1)}, u32[]{:S(2)}, u32[]{:S(2)}) collective-permute-start(f32[16,1024]{1,0:T(8,128)S(1)} %get-tuple-element.13), channel_id=1, source_target_pairs={{0,32},{32,0},{64,96},{96,64},{128,160},{160,128},{192,224},{224,1... | collective-permute-start | bytes 196616 | tf_op jit(solution)/shard_map/ppermute | solution.py:187
  7.2 12.0 %copy-start.7 = (f32[264,32]{1,0:T(8,128)S(1)}, f32[264,32]{1,0:T(8,128)}, u32[]{:S(2)}) copy-start(f32[264,32]{1,0:T(8,128)} %constant.51.clone.receive) | copy-start | bytes 101380
  7.2 12.0 %collective-permute-start.1 = (f32[16,1024]{1,0:T(8,128)S(1)}, f32[16,1024]{1,0:T(8,128)S(1)}, u32[]{:S(2)}, u32[]{:S(2)}) collective-permute-start(f32[16,1024]{1,0:T(8,128)S(1)} %get-tuple-element.14), channel_id=1, source_target_pairs={{0,224},{32,64},{64,32},{96,128},{128,96},{160,192},{192,160},{224... | collective-permute-start | bytes 196616 | tf_op jit(solution)/shard_map/ppermute | solution.py:187
  21.2 16.1 %collective-permute-start.3 = (f32[8,2048]{1,0:T(8,128)S(1)}, f32[8,2048]{1,0:T(8,128)S(1)}, u32[]{:S(2)}, u32[]{:S(2)}) collective-permute-start(f32[8,2048]{1,0:T(8,128)S(1)} %get-tuple-element.16), channel_id=1, source_target_pairs={{0,31},{1,2},{2,1},{3,4},{4,3},{5,6},{6,5},{7,8},{8,7},{9,10},{10,... | collective-permute-start | bytes 196616 | tf_op jit(solution)/shard_map/ppermute | solution.py:187
  23.4 13.9 %collective-permute-start.2 = (f32[8,2048]{1,0:T(8,128)S(1)}, f32[8,2048]{1,0:T(8,128)S(1)}, u32[]{:S(2)}, u32[]{:S(2)}) collective-permute-start(f32[8,2048]{1,0:T(8,128)S(1)} %get-tuple-element.16), channel_id=1, source_target_pairs={{0,1},{1,0},{2,3},{3,2},{4,5},{5,4},{6,7},{7,6},{8,9},{9,8},{10,11... | collective-permute-start | bytes 196616 | tf_op jit(solution)/shard_map/ppermute | solution.py:187
  29.7 7.6 %copy-start.4 = (f32[768,128]{1,0:T(8,128)S(1)}, f32[768,128]{1,0:T(8,128)}, u32[]{:S(2)}) copy-start(f32[768,128]{1,0:T(8,128)} %constant.54.clone.y_table) | copy-start | bytes 1179652
  29.7 7.7 %copy-start.5 = (f32[256,264]{1,0:T(8,128)S(1)}, f32[256,264]{1,0:T(8,128)}, u32[]{:S(2)}) copy-start(f32[256,264]{1,0:T(8,128)} %constant.53.clone.x_table) | copy-start | bytes 811012
  29.7 7.7 %copy-start.8 = (f32[128,256]{1,0:T(8,128)S(1)}, f32[128,256]{1,0:T(8,128)}, u32[]{:S(2)}) copy-start(f32[128,256]{1,0:T(8,128)} %constant.55.clone.spread) | copy-start | bytes 393220
  29.7 7.7 %copy-start.9 = (f32[16,256]{1,0:T(8,128)S(1)}, f32[16,256]{1,0:T(8,128)}, u32[]{:S(2)}) copy-start(f32[16,256]{1,0:T(8,128)} %constant.52.clone.receive) | copy-start | bytes 49156
  35.3 2.0 %copy-start.1 = (f32[8,512,256]{2,1,0:T(8,128)}, f32[8,512,256]{2,1,0:T(8,128)S(1)}, u32[]{:S(2)}) copy-start(f32[8,512,256]{2,1,0:T(8,128)S(1)} %details.1.w) | copy-start | bytes 12582916
where the time goes:
time: 45.7 us; the launch traced here: 45.4 us
  Pallas kernels  26.2 us (57%)
  starting transfers between devices  13.4 us (29%)
  local copies, waits for them, and re-layouts  5.6 us (12%)
    ppermute x4, starting transfers between devices, swap(): return (lax.ppermute(first, axis, inner), lax.ppermute(second, axis, outer))  13.4 us
    pallas_call x1, Pallas kernels, shards(): pl.pallas_call(functools.partial(own_kernel, z_a, z_d), out_shape=(shape(...  9.38 us
    pallas_call x1, Pallas kernels, shards(): pl.pallas_call(functools.partial(last_kernel, z2_a, z2_d), out_shape=shap...  8.06 us
    pallas_call x1, Pallas kernels, shards(): pl.pallas_call(detail_kernel, out_shape=shape(planes, fine, width), in_sp...  5.66 us
    unnamed x24, local copies, waits for them, and re-layouts  5.6 us
    pallas_call x1, Pallas kernels, shards(): pl.pallas_call(join_kernel, out_shape=(shape(half, rows, width), shape(8,...  2.06 us
    pallas_call x1, Pallas kernels, shards(): pl.pallas_call(functools.partial(edge_kernel, z_a, z_d), out_shape=(shape...  1.08 us
  transfers between devices with their start and end apart: 4, of which 0 were waited for; matrix products, arithmetic and copies ran while one was open for 0% of the time, Pallas kernels for 33%

commit v1 on v0

v1 whole, which is shorter than its diff:
```python
import functools

import jax
import jax.numpy as jnp
import numpy as np
from jax import lax
from jax.experimental import pallas as pl
from jax.experimental.pallas import tpu as pltpu
from jax.sharding import PartitionSpec as P

ROOT = np.sqrt(3.0) - 2.0
CENTRE = 3.0 / np.sqrt(12.0)
F32 = jnp.float32


def line_operators(fine):
    n = fine // 2
    load = np.zeros((3 * n, 3 * fine))
    even = np.zeros((3 * n, 3 * n))
    for j in range(3 * n):
        for at, weight in ((2 * j, 1 / 3), (2 * j - 2, -1 / 6), (2 * j + 2, -1 / 6),
                           (2 * j - 1, 0.5), (2 * j + 1, 0.5)):
            if 0 <= at < 3 * fine:
                load[j, at] = weight
        for at, weight in ((j, 5 / 6), (j - 1, 1 / 12), (j + 1, 1 / 12)):
            if 0 <= at < 3 * n:
                even[j, at] = weight
    place = np.arange(3 * n)
    solve = CENTRE * ROOT ** np.abs(place[:, None] - place[None, :])
    a = (solve @ load)[:, fine:2 * fine]
    d = (solve @ even)[:, n:2 * n]
    near = np.arange(n)
    return dict(
        n=n, a=a[n:2 * n], a_left=a[n - 1], a_right=a[2 * n],
        d=d[n:2 * n], d_left=d[n - 1], d_right=d[2 * n],
        from_left=ROOT ** near, from_right=ROOT ** (n - 1 - near),
    )


def on_even(rows):
    wide = np.zeros(rows.shape[:-1] + (2 * rows.shape[-1],))
    wide[..., ::2] = rows
    return wide


def two_levels(fine):
    one = line_operators(fine)
    two = line_operators(one["n"])
    functionals = dict(
        a_left=two["a_left"], a_right=two["a_right"],
        d_left=on_even(two["d_left"]), d_right=on_even(two["d_right"]),
    )
    return one, two, functionals


def pieces(table, axis):
    high = table.astype(jnp.bfloat16)
    low = (table - high.astype(np.float64)).astype(jnp.bfloat16)
    return np.concatenate([high, low, high], axis)


def cut(data, axis):
    high = data.astype(jnp.bfloat16)
    low = (data - high.astype(F32)).astype(jnp.bfloat16)
    return jnp.concatenate([high, high, low], axis)


def dot(a, b, dims=((1,), (0,))):
    return lax.dot_general(a, b, (dims, ((), ())), preferred_element_type=F32)


def x_tables(fine):
    one, two, f = two_levels(fine)
    n = one["n"]
    rows = n + 16
    own = []
    for kind in ("a", "d"):
        table = np.zeros((rows, one[kind].shape[1]))
        left, right = one[kind + "_left"], one[kind + "_right"]
        table[:n] = one[kind]
        table[n] = right
        table[n + 1] = (f["a_right"] @ one["from_right"]) * left
        table[n + 2] = (f["a_left"] @ one["from_left"]) * right
        table[n + 3] = (f["d_right"] @ one["from_right"]) * left
        table[n + 4] = (f["d_left"] @ one["from_left"]) * right
        own.append(table)
    send = []
    for side in ("left", "right"):
        part = np.zeros((16, fine))
        for base, step, kind in ((0, 1, "a"), (4, 2, "d")):
            part[base, ::step] = one[kind + "_" + side]
            part[base + 1, ::step] = f["a_" + side] @ one[kind]
            part[base + 2, ::step] = f["d_" + side] @ one[kind]
            part[base + 3, ::step] = one[kind][0]
        part[8], part[9] = on_even(f["a_" + side]), on_even(f["d_" + side])
        send.append(part)
    receive = np.zeros((rows, 32))
    for base in (0, 4):
        receive[:n, base] = one["from_left"]
        receive[n + 1, base + 1] = 1
        receive[n + 3, base + 2] = 1
        receive[:n, 16 + base] = one["from_right"]
        receive[n + 2, 16 + base + 1] = 1
        receive[n + 4, 16 + base + 2] = 1
        receive[n, 16 + base + 3] = 1
    receive[n + 1, 8] = receive[n + 3, 9] = 1
    receive[n + 2, 16 + 8] = receive[n + 4, 16 + 9] = receive[n, 16 + 10] = 1
    m = n // 2
    level2_a, level2_d = np.zeros((m, rows)), np.zeros((m, rows))
    level2_a[:, :n], level2_d[:, :n] = two["a"], on_even(two["d"])
    level2_a[:, n + 1], level2_a[:, n + 2] = two["from_left"], two["from_right"]
    level2_d[:, n + 3], level2_d[:, n + 4] = two["from_left"], two["from_right"]
    return own, send, receive, level2_a, level2_d


SENT = dict(zip(("left", "right", "a_left", "a_right", "d_left", "d_right", "first"),
                (9, 1, 11, 3, 13, 5, 15)))
MESSAGE_ROW = dict(zip(SENT, range(7)))
MOMENTS = (17, 19, 21, 23)


def y_tables(fine):
    one, two, f = two_levels(fine)
    n = one["n"]

    def fill(table, inside, left, right):
        table[:, ::2] = inside.T
        table[:, fine - 1] = right
        table[:, MOMENTS[0]] = (f["a_right"] @ one["from_right"]) * left
        table[:, MOMENTS[1]] = (f["a_left"] @ one["from_left"]) * right
        table[:, MOMENTS[2]] = (f["d_right"] @ one["from_right"]) * left
        table[:, MOMENTS[3]] = (f["d_left"] @ one["from_left"]) * right
        table[:, SENT["left"]], table[:, SENT["right"]] = left, right
        for name in ("a_left", "a_right", "d_left", "d_right"):
            table[:, SENT[name]] = f[name] @ inside
        table[:, SENT["first"]] = inside[0]
        return table

    a = fill(np.zeros((fine, fine)), one["a"], one["a_left"], one["a_right"])
    d = fill(np.zeros((n, fine)), one["d"], one["d_left"], one["d_right"])
    e = fill(np.zeros((n, fine)), np.eye(n), np.zeros(n), np.zeros(n))
    e[:, ::2] = 0
    both = np.zeros((fine, fine))
    both[::2], both[1::2] = -d, e
    receive = np.zeros((16, fine))
    at = MESSAGE_ROW
    receive[at["right"], ::2] = one["from_left"]
    receive[at["a_right"], MOMENTS[0]] = receive[at["d_right"], MOMENTS[2]] = 1
    receive[8 + at["left"], ::2] = one["from_right"]
    receive[8 + at["a_left"], MOMENTS[1]] = receive[8 + at["d_left"], MOMENTS[3]] = 1
    receive[8 + at["first"], fine - 1] = 1
    level2_a, level2_d = np.zeros((fine, n // 2)), np.zeros((fine, n // 2))
    level2_a[::2], level2_d[::2] = two["a"].T, -on_even(two["d"]).T
    level2_a[MOMENTS[0]], level2_a[MOMENTS[1]] = two["from_left"], two["from_right"]
    level2_d[MOMENTS[2]], level2_d[MOMENTS[3]] = -two["from_left"], -two["from_right"]
    level2_a, level2_d = on_even(on_even(level2_a)), on_even(on_even(level2_d))
    predict = np.zeros((fine, fine))
    for j in range(0, fine, 2):
        predict[j, j] = 1
        if j % 4:
            predict[j - 2, j] = predict[(j + 2) if j + 2 < fine else fine - 1, j] = -0.5
    updates = [receive @ predict, receive @ level2_a, receive @ level2_d]
    return a, both, level2_a, level2_d, updates


def z_tables(planes):
    n = planes // 2
    predict, spread = np.eye(planes), np.zeros((planes, n))
    mass, restrict, solve = (np.zeros(s) for s in ((planes, planes), (n, planes), (n, n)))
    for i in range(planes):
        for at, weight in ((i, 4 / 6), (i - 1, 1 / 6), (i + 1, 1 / 6)):
            mass[i, at % planes] += weight
        if i % 2:
            predict[i, i - 1] -= 0.5
            predict[i, (i + 1) % planes] -= 0.5
    for j in range(n):
        spread[2 * j, j] = 1
        for at, weight in ((2 * j, 1.0), (2 * j - 1, 0.5), (2 * j + 1, 0.5)):
            restrict[j, at % planes] += weight
        for at, weight in ((j, 4 / 3), (j - 1, 1 / 3), (j + 1, 1 / 3)):
            solve[j, at % n] += weight
    load = np.linalg.inv(solve) @ restrict @ mass
    return (load @ predict).tolist(), (load @ spread).tolist()


def pack(arrays, width):
    blocks, places, start = [], [], 0
    for array in arrays:
        rows, columns = array.shape
        count = -(-columns // width)
        padded = np.pad(array, ((0, 0), (0, count * width - columns)))
        blocks += [padded[:, k * width:(k + 1) * width] for k in range(count)]
        places.append((start, rows, columns))
        start += rows * count
    return np.concatenate(blocks, 0), tuple(places)


def unpack(table, place):
    start, rows, columns = place
    width = table.shape[1]
    count = -(-columns // width)
    blocks = [table[start + k * rows:start + (k + 1) * rows, :] for k in range(count)]
    whole = blocks[0] if count == 1 else jnp.concatenate(blocks, 1)
    return whole if columns == count * width else whole[:, :columns]


def combine(weights, planes):
    total = None
    for weight, plane in zip(weights, planes):
        term = plane * float(weight)
        total = term if total is None else total + term
    return total


def exchange(to_left, to_right, axis):
    size = lax.axis_size(axis)
    forward = [(i, (i + 1) % size) for i in range(size)]
    backward = [(target, source) for source, target in forward]
    right = lax.ppermute(to_left, axis, backward)
    return lax.ppermute(to_right, axis, forward), right


def iota(shape, dimension):
    return lax.broadcasted_iota(jnp.int32, shape, dimension)


def edge_weights(table, shape, reverse):
    near = table[:, ::-1] if reverse else table
    row, lane = iota(shape, 0), iota(shape, 1)
    place = (shape[1] - 1 - lane) if reverse else lane
    group = place // 4
    sign = jnp.where(group % 2 == 1, -1.0, 1.0)
    one = jnp.exp(group.astype(F32) * float(np.log(-ROOT)))
    slow, fast = sign * one, one * one
    total = jnp.zeros(shape, F32)
    for phase in range(4):
        some = near[:, phase::4]
        basis = np.stack([ROOT ** np.arange(1, 5), ROOT ** (2 * np.arange(1, 5))], 1)
        factors = np.linalg.lstsq(basis, some[:, 1:5].T, rcond=None)[0]
        here = place % 4 == phase
        first = jnp.zeros(shape, F32)
        rest_slow, rest_fast = jnp.zeros(shape, F32), jnp.zeros(shape, F32)
        for k in range(table.shape[0]):
            if np.any(some[k]):
                mine = row == k
                first = jnp.where(mine, float(some[k, 0]), first)
                rest_slow = jnp.where(mine, float(factors[0, k]), rest_slow)
                rest_fast = jnp.where(mine, float(factors[1, k]), rest_fast)
        rest = rest_slow * slow + rest_fast * fast
        total = jnp.where(here, jnp.where(group == 0, first, rest), total)
    return total


def edge_kernel(tables, z_a, z_d, u, to_left, to_right, strips, arrived):
    _, planes, halves, depth, lanes = strips.shape
    fine = u.shape[1]
    copies = [
        [
            pltpu.make_async_copy(
                u.at[:, pl.ds(start, depth), pl.ds(h * lanes, lanes)],
                strips.at[side, :, h],
                arrived.at[side, h],
            )
            for h in range(halves)
        ]
        for side, start in ((0, 0), (1, fine - depth))
    ]
    for band in copies:
        for copy in band:
            copy.start()
    weights = []
    for side in range(2):
        weight = edge_weights(tables[side], (16, depth), side == 1)
        high = weight.astype(jnp.bfloat16)
        low = (weight - high.astype(F32)).astype(jnp.bfloat16)
        weights.append(jnp.concatenate([high, low, high], 1))

    def message(side):
        for copy in copies[side]:
            copy.wait()
        tiles = [strips[side, k, h] for k in range(planes) for h in range(halves)]
        data = jnp.concatenate(tiles, 1)
        width = halves * lanes
        sums = dot(weights[side], cut(data, 0))
        plane = [sums[:, k * width:(k + 1) * width] for k in range(planes)]
        index = iota(plane[0].shape, 0)
        out = []
        for z in range(planes // 2):
            a, d = combine(z_a[z], plane), combine(z_d[z], plane[::2])
            part = jnp.where(index < 4, a, jnp.where(index < 8, d, plane[2 * z]))
            if side == 0:
                even = data[:1, 2 * z * width:(2 * z + 1) * width]
                odd = data[:1, (2 * z + 1) * width:(2 * z + 2) * width]
                part = jnp.where(index == 10, even, jnp.where(index == 11, odd, part))
            out.append(part)
        return jnp.concatenate(out, 1)

    to_left[...] = message(0)
    to_right[...] = message(1)


def own_kernel(z_a, z_d, reach, places, block, table, c, side, column, u, arrived):
    planes, halves, fine, lanes = u.shape
    part = fine // 2
    copies = [
        [
            pltpu.make_async_copy(
                block.at[:, pl.ds(at * part, part), pl.ds(h * lanes, lanes)],
                u.at[:, h, pl.ds(at * part, part), :],
                arrived.at[at, h],
            )
            for h in range(halves)
        ]
        for at in range(2)
    ]
    for some in copies:
        for copy in some:
            copy.start()
    n, rows, stride = fine // 2, c.shape[1], side.shape[1] // c.shape[0]
    join = lambda parts: jnp.concatenate(parts, 1)
    tables = [unpack(table, place) for place in places]
    y_table = tables[4]
    even, x_parts = [], []
    for at in range(2):
        for copy in copies[at]:
            copy.wait()
        whole = [
            join([u[k, h, at * part:(at + 1) * part, :] for h in range(halves)])
            for k in range(planes)
        ]
        even.append([
            join([u[k, h, pl.ds(at * part, part // 2, stride=2), :] for h in range(halves)])
            for k in range(0, planes, 2)
        ])
        x_parts.append([
            [
                dot(tables[2 * at], cut(combine(z_a[z], whole), 0)),
                dot(tables[2 * at + 1], cut(combine(z_d[z], even[at]), 0)),
            ]
            for z in range(planes // 2)
        ])

    def whole_rows(low, high):
        middle, edge = n // 2 - reach, n // 2 + reach
        return jnp.concatenate([
            low[:middle], low[middle:edge] + high[:2 * reach], high[2 * reach:edge],
            low[edge:] + high[edge:],
        ], 0)

    for z in range(planes // 2):
        x_a = whole_rows(x_parts[0][z][0], x_parts[1][z][0])
        x_d = whole_rows(x_parts[0][z][1], x_parts[1][z][1])
        odd_lane = iota(x_d.shape, 1) % 2 == 1
        field = jnp.concatenate([even[0][z], even[1][z], jnp.zeros((rows - n, halves * lanes), F32)], 0)
        x_de = jnp.where(odd_lane, pltpu.roll(field, 1, 1), x_d)
        total = dot(join([cut(x_a, 1), cut(x_de, 1)]), y_table)
        total = total + jnp.where(odd_lane, 0.0, field)
        c[z] = total
        turned = total[:, :lanes].T
        index = iota((8, rows), 0)
        kept = jnp.where(index % 2 == 1, turned[:8], pltpu.roll(turned[8:16], 7, 0))
        side[:, z * stride:z * stride + rows] = kept
        if stride > rows:
            side[:, z * stride + rows:(z + 1) * stride] = jnp.zeros((8, stride - rows), F32)
    for k in range(planes):
        column[k:k + 1, :] = u[k, 0].T[:1, :]


def typed_rows(from_left, from_right, half):
    both = jnp.concatenate([from_left, from_right], 0)
    width = both.shape[1] // half
    rows = jnp.concatenate([both[:, z * width:(z + 1) * width] for z in range(half)], 0)
    kind = iota(rows.shape, 0) % 16
    even_lane = iota(rows.shape, 1) % 2 == 0
    field = jnp.where((kind >= 8) & (kind <= 10) & even_lane, rows, 0.0)
    a = jnp.where(kind < 4, rows, 0.0)
    d = jnp.where((kind >= 4) & (kind < 8) & even_lane, rows, 0.0)
    return jnp.concatenate([cut(a, 1), cut(d + pltpu.roll(field, 1, 1), 1)], 1), field


def join_kernel(half, side, column, left, right, y_sent, receive, message, again):
    from_left, from_right = left[...], right[...]
    typed, _ = typed_rows(from_left, from_right, half)
    sums = dot(y_sent[...], typed, ((1,), (1,)))[:8]
    part = iota(sums.shape, 1) // 32
    spread = jnp.concatenate([jnp.where(part == z, sums, 0.0) for z in range(half)], 0)
    added = dot(cut(spread, 1), receive[...])
    stride = side.shape[1] // half
    for z in range(half):
        here = slice(z * stride, (z + 1) * stride)
        message[:, here] = side[:, here] + added[8 * z:8 * z + 8]
    u0 = column[...]
    fine = u0.shape[1]
    width = from_right.shape[1] // half
    plane, lane = iota(u0.shape, 0), iota(u0.shape, 1)
    after = pltpu.roll(u0, fine - 1, 1)
    for z in range(half):
        for k, row in ((2 * z, 10), (2 * z + 1, 11)):
            corner = from_right[row:row + 1, z * width:z * width + 1]
            after = jnp.where((plane == k) & (lane == fine - 1), corner, after)
    before = pltpu.roll(u0, 1, 1)
    u0 = jnp.where(lane % 2 == 1, u0 - 0.5 * (before + after), u0)
    around = pltpu.roll(u0, 1, 0) + pltpu.roll(u0, 2 * half - 1, 0)
    message[:, half * stride:] = jnp.where(plane % 2 == 1, u0 - 0.5 * around, u0)
    again[...] = message[...]


def middle_kernel(
    z_a, z_d, places, c_own, block, left, right, table, out, w, edge, u, inner, ready, arrived, sent
):
    planes, halves, fine, lanes = u.shape
    copies = [
        pltpu.make_async_copy(block.at[:, :, pl.ds(h * lanes, lanes)], u.at[:, h], arrived.at[h])
        for h in range(halves)
    ]
    for copy in copies:
        copy.start()
    half, rows, width = c_own.shape
    n, quarter = fine // 2, fine // 4
    from_left, from_right = left[...], right[...]
    typed, field = typed_rows(from_left, from_right, half)
    y_table, receive, x_level2, y_level2 = (unpack(table, place) for place in places)
    processed = dot(typed, y_table) + field
    lane = iota((rows, width), 1)
    row = iota((rows, width), 0)
    coarse, details = [], []
    for z in range(half):
        c = c_own[z] + dot(receive, cut(processed[32 * z:32 * z + 32], 0))
        coarse.append(c)
        around = pltpu.roll(c, 1, 0) + pltpu.roll(c, rows - 1, 0)
        c = jnp.where(row % 2 == 1, c - 0.5 * around, c)[:n]
        after = pltpu.roll(c, width - 2, 1)
        after = jnp.where(lane[:n] == width - 2, pltpu.roll(c, width - 1, 1), after)
        around = pltpu.roll(c, 2, 1) + after
        details.append(jnp.where(lane[:n] % 4 == 2, c - 0.5 * around, c))
    level = [dot(x_level2, cut(c, 0)) for c in coarse]
    level_a = [part[:quarter] for part in level]
    level_d = [part[quarter:] for part in level[::2]]
    for z in range(half):
        values = details[z]
        if z % 2:
            values = values - 0.5 * (details[z - 1] + details[(z + 1) % half])
        for h in range(halves):
            inner[z, h] = values[:, h * lanes:(h + 1) * lanes]
        if z % 2 == 0:
            a, d = combine(z_a[z // 2], level_a), combine(z_d[z // 2], level_d)
            added = dot(jnp.concatenate([cut(a, 1), cut(d, 1)], 1), y_level2)
            for h in range(halves):
                here = (z, h, pl.ds(0, quarter, stride=2), slice(None))
                inner[here] = inner[here] + added[:, h * lanes:(h + 1) * lanes]

    for copy in copies:
        copy.wait()
    last_row = iota((n, width), 0) == n - 1
    even_lane = iota((n, width), 1) % 2 == 0

    def rows_of(k):
        load = lambda start: jnp.concatenate(
            [u[k, h, pl.ds(start, n, stride=2), :] for h in range(halves)], 1
        )
        even, odd = load(0), load(1)
        at = (k // 2) * width
        halo = from_right[10 + k % 2:11 + k % 2, at:at + width]
        after = jnp.where(last_row, halo, pltpu.roll(even, n - 1, 0))
        return even, odd - 0.5 * (even + after)

    def along_y(part):
        after = jnp.where(iota(part.shape, 1) == width - 1, 0.0, pltpu.roll(part, width - 1, 1))
        return jnp.where(even_lane, part, part - 0.5 * (pltpu.roll(part, 1, 1) + after))

    def store(k, start, part):
        for h in range(halves):
            target = w.at[k // 2, h] if k % 2 == 0 else (
                edge.at[k // 2] if h == halves - 1 else ready.at[k // 2, h])
            target[pl.ds(start, n, stride=2), :] = part[:, h * lanes:(h + 1) * lanes]

    begin = rows_of(0)
    here, done = begin, []
    for k in range(0, planes, 2):
        held = jnp.concatenate([inner[k // 2, h] for h in range(halves)], 1)
        store(k, 0, jnp.where(even_lane, held, along_y(here[0])))
        store(k, 1, along_y(here[1]))
        following = begin if k + 2 == planes else rows_of(k + 2)
        between = rows_of(k + 1)
        for start in (0, 1):
            store(k + 1, start, along_y(between[start] - 0.5 * (here[start] + following[start])))
        for h in range(halves - 1):
            copy = pltpu.make_async_copy(
                ready.at[k // 2, h], out.at[k + 1, :, pl.ds(h * lanes, lanes)], sent.at[k // 2, h]
            )
            copy.start()
            done.append(copy)
        here = following
    for copy in done:
        copy.wait()


def last_kernel(
    z_a, z_d, left, right, x_level2, updates, w, edge, started, out, done, finished, sent
):
    half, halves, fine, lanes = w.shape
    n = fine // 2
    stride = (left.shape[1] - fine) // half
    from_left, from_right = left[...], right[...]
    column = from_right[:, half * stride:].T
    last = iota((fine, lanes), 1) == lanes - 1
    copies = []

    def send(source, k, h):
        copy = pltpu.make_async_copy(source, out.at[k, :, pl.ds(h * lanes, lanes)], sent.at[k, h])
        copy.start()
        copies.append(copy)

    def finish(values, k):
        return jnp.where(last, values - 0.5 * column[:, k:k + 1], values)

    for z in range(half):
        finished[z] = finish(edge[z], 2 * z + 1)
        send(finished.at[z], 2 * z + 1, halves - 1)
        for h in range(halves):
            done[z, h] = finish(w[z, h], 2 * z) if h == halves - 1 else w[z, h]
    both = jnp.concatenate([from_left, from_right], 0)
    sides = [both[:, z * stride:(z + 1) * stride] for z in range(half)]
    level = dot(cut(jnp.concatenate(sides, 0), 1), x_level2[...])
    lane = iota(sides[0].shape, 1)
    details = []
    for side in sides:
        around = pltpu.roll(side, 1, 1) + pltpu.roll(side, stride - 1, 1)
        details.append(jnp.where(lane % 2 == 1, side - 0.5 * around, side)[:, :n])
    quarter = n // 2
    level_a = [level[16 * z:16 * z + 16, :quarter] for z in range(half)]
    level_d = [level[16 * z:16 * z + 16, quarter:] for z in range(0, half, 2)]

    def update(factor, start):
        stop = start + factor.shape[0]
        table = jnp.concatenate([updates[piece, start:stop] for piece in range(3)], 0)
        return dot(cut(factor, 0), table, ((0,), (0,)))

    for z in range(half):
        if z % 2:
            factor = details[z] - 0.5 * (details[z - 1] + details[(z + 1) % half])
        else:
            factor = details[z]
            parts = [combine(z_a[z // 2], level_a), combine(z_d[z // 2], level_d)]
            coarse = update(jnp.concatenate(parts, 0), 16)
        added = update(factor, 0)
        for h in range(halves):
            here = (z, h, pl.ds(0, n, stride=2), slice(None))
            done[here] = done[here] + added[:, h * lanes:(h + 1) * lanes]
            if z % 2 == 0:
                here = (z, h, pl.ds(0, quarter, stride=4), slice(None))
                done[here] = done[here] + coarse[:, h * lanes:(h + 1) * lanes]
            send(done.at[z, h], 2 * z, h)
    for copy in copies:
        copy.wait()


def shards(density):
    planes, fine, width = density.shape
    half, n, lanes = planes // 2, fine // 2, 128
    halves = width // lanes
    depth = min(64, fine)
    z_a, z_d = z_tables(planes)
    z2_a, z2_d = z_tables(half)
    (own_a, own_d), send, x_receive, x2_a, x2_d = x_tables(fine)
    y_a, y_de, y2_a, y2_d, updates = y_tables(width)
    rows = n + 16
    stride = -(-rows // 128) * 128
    y_table = np.concatenate([pieces(y_a, 0), pieces(y_de, 0)], 0)
    sent = list(SENT.values())
    y_sent = np.zeros((16, y_table.shape[0]), y_table.dtype)
    y_sent[:len(sent)] = y_table[:, sent].T
    x_receive_t = np.zeros((32, stride))
    x_receive_t[:, :rows] = x_receive.T
    x2_t = np.zeros((stride, n))
    x2_t[:rows] = np.concatenate([x2_a.T, x2_d.T], 1)
    update = np.concatenate(updates, 0)
    high = update.astype(jnp.bfloat16)
    low = (update - high.astype(np.float64)).astype(jnp.bfloat16)
    params = lambda mib: pltpu.CompilerParams(vmem_limit_bytes=mib * 2**20)
    vmem = pl.BlockSpec(memory_space=pltpu.VMEM)
    hbm = pl.BlockSpec(memory_space=pltpu.HBM)
    shape = lambda *dims: jax.ShapeDtypeStruct(dims, F32)

    to_left, to_right = pl.pallas_call(
        functools.partial(edge_kernel, (send[0][:, :depth], send[1][:, fine - depth:]), z_a, z_d),
        out_shape=(shape(16, half * width),) * 2,
        in_specs=[hbm],
        out_specs=[vmem] * 2,
        scratch_shapes=[
            pltpu.VMEM((2, planes, halves, depth, lanes), F32),
            pltpu.SemaphoreType.DMA((2, halves)),
        ],
        compiler_params=params(50),
        name="edges",
    )(density)
    left_x, right_x = exchange(to_left, to_right, "gx")

    reach = min(16, n // 2)
    tail = list(range(n, rows))
    front = list(range(n // 2 + reach)) + tail
    back = list(range(n // 2 - reach, n)) + tail
    packed, places = pack(
        [
            pieces(own_a[front][:, :n], 1), pieces(own_d[front][:, :n // 2], 1),
            pieces(own_a[back][:, n:], 1), pieces(own_d[back][:, n // 2:], 1),
            y_table,
        ],
        width,
    )
    c_own, side, column = pl.pallas_call(
        functools.partial(own_kernel, z_a, z_d, reach, places),
        out_shape=(shape(half, rows, width), shape(8, half * stride), shape(planes, fine)),
        in_specs=[hbm, vmem],
        out_specs=[vmem] * 3,
        scratch_shapes=[
            pltpu.VMEM((planes, halves, fine, lanes), F32),
            pltpu.SemaphoreType.DMA((2, halves)),
        ],
        compiler_params=params(50),
        name="own",
    )(density, packed)

    to_left, to_right = pl.pallas_call(
        functools.partial(join_kernel, half),
        out_shape=(shape(8, half * stride + fine),) * 2,
        in_specs=[vmem] * 6,
        out_specs=[vmem] * 2,
        compiler_params=params(8),
        name="join",
    )(side, column, left_x, right_x, y_sent, pieces(np.tile(x_receive_t, (half, 1)), 0))
    left_y, right_y = exchange(to_left, to_right, "gy")

    x_level2 = pieces(np.concatenate([x2_a, x2_d], 0), 1)
    y_level2 = np.concatenate([pieces(y2_a, 0), pieces(y2_d, 0)], 0)
    packed, places = pack([y_table, pieces(x_receive, 1), x_level2, y_level2], width)
    started, w, edge = pl.pallas_call(
        functools.partial(middle_kernel, z2_a, z2_d, places),
        out_shape=(
            shape(planes, fine, width), shape(half, halves, fine, lanes), shape(half, fine, lanes),
        ),
        in_specs=[vmem, hbm, vmem, vmem, vmem],
        out_specs=[hbm, vmem, vmem],
        scratch_shapes=[
            pltpu.VMEM((planes, halves, fine, lanes), F32),
            pltpu.VMEM((half, halves, n, lanes), F32),
            pltpu.VMEM((half, halves - 1, fine, lanes), F32),
            pltpu.SemaphoreType.DMA((halves,)),
            pltpu.SemaphoreType.DMA((half, halves - 1)),
        ],
        compiler_params=params(44),
        name="middle",
    )(c_own, density, left_x, right_x, packed)

    return pl.pallas_call(
        functools.partial(last_kernel, z2_a, z2_d),
        out_shape=shape(planes, fine, width),
        in_specs=[vmem] * 6 + [hbm],
        out_specs=hbm,
        scratch_shapes=[
            pltpu.VMEM((half, halves, fine, lanes), F32),
            pltpu.VMEM((half, fine, lanes), F32),
            pltpu.SemaphoreType.DMA((planes, halves)),
        ],
        input_output_aliases={6: 0},
        compiler_params=params(16),
        name="last",
    )(left_y, right_y, pieces(x2_t, 0), np.stack([high, low, high]), w, edge, started)


def solution(mesh):
    spec = P(None, "gx", "gy")
    return jax.shard_map(shards, mesh=mesh, in_specs=(spec,), out_specs=spec, check_vma=False)
```

time: 45.7 us -> 26.5 us (0.58)
  the two profiles are of different devices: /device:TPU:1 before, /device:TPU:71 now
where the time goes in v1:
time: 26.5 us; the launch traced here: 26.4 us
  Pallas kernels  15.2 us (57%)
  starting transfers between devices  8.97 us (34%)
  waiting for transfers between devices  2.16 us (8%)
    ppermute x2, starting transfers between devices, exchange(): return (lax.ppermute(to_right, axis, forward), right)  6.4 us
    pallas_call x1, Pallas kernels, shards(): pl.pallas_call(functools.partial(middle_kernel, z2_a, z2_d, places), out_...  5.72 us
    pallas_call x1, Pallas kernels, shards(): pl.pallas_call(functools.partial(own_kernel, z_a, z_d, reach, places), ou...  4.68 us
    pallas_call x1, Pallas kernels, shards(): pl.pallas_call(functools.partial(last_kernel, z2_a, z2_d), out_shape=shap...  2.66 us
    ppermute x2, starting transfers between devices, exchange(): right = lax.ppermute(to_left, axis, backward)  2.57 us
    ppermute x2, waiting for transfers between devices, exchange(): right = lax.ppermute(to_left, axis, backward)  2.16 us
    pallas_call x1, Pallas kernels, shards(): pl.pallas_call(functools.partial(edge_kernel, (send[0][:, :depth], send[1...  1.66 us
  transfers between devices with their start and end apart: 4, of which 1 were waited for; matrix products, arithmetic and copies ran while one was open for 0% of the time, Pallas kernels for 39%

profile of v1, /device:TPU:71, one launch (start us, length us, event | category | flops | bytes accessed | tf_op | source)
XLA Modules:
  0.0 26.4 jit_solution(2789600716162817911)
XLA Ops:
  0.0 0.0 copy-start.1
  0.0 1.7 %edges.1 = (f32[16,1024]{1,0:T(8,128)S(1)}, f32[16,1024]{1,0:T(8,128)S(1)}) custom-call(f32[8,512,256]{2,1,0:T(8,128)} %block.3), custom_call_target="tpu_custom_call" | custom-call | tf_op jit(solution)/shard_map/edges/pallas_call | solution.py:585
  1.7 1.7 %collective-permute-start = (f32[16,1024]{1,0:T(8,128)S(1)}, f32[16,1024]{1,0:T(8,128)S(1)}, u32[]{:S(2)}, u32[]{:S(2)}) collective-permute-start(f32[16,1024]{1,0:T(8,128)S(1)} %get-tuple-element.17), channel_id=1, source_target_pairs={{0,32},{32,64},{64,96},{96,128},{128,160},{160,192},{192,224},{224... | collective-permute-start | bytes 196616 | tf_op jit(solution)/shard_map/ppermute | solution.py:220
  3.4 0.0 copy-start.3
  3.4 0.0 copy-start.5
  3.4 0.0 copy-start
  3.4 2.6 %collective-permute-start.1 = (f32[16,1024]{1,0:T(8,128)S(1)}, f32[16,1024]{1,0:T(8,128)S(1)}, u32[]{:S(2)}, u32[]{:S(2)}) collective-permute-start(f32[16,1024]{1,0:T(8,128)S(1)} %get-tuple-element.18), channel_id=1, source_target_pairs={{32,0},{64,32},{96,64},{128,96},{160,128},{192,160},{224,192},{0,2... | collective-permute-start | bytes 196616 | tf_op jit(solution)/shard_map/ppermute | solution.py:219
  6.0 0.0 copy-done.1
  6.0 4.7 %own.1 = (f32[4,272,256]{2,1,0:T(8,128)S(1)}, f32[8,1536]{1,0:T(8,128)S(1)}, f32[8,512]{1,0:T(8,128)S(1)}) custom-call(f32[8,512,256]{2,1,0:T(8,128)} %block.3, bf16[3136,256]{1,0:T(8,128)(2,1)S(1)} %copy-done.1), custom_call_target="tpu_custom_call" | custom-call | tf_op jit(solution)/shard_map/own/pallas_call | solution.py:611
  10.7 0.0 collective-permute-done.left
  10.7 0.0 collective-permute-done.1.right
  10.7 0.0 copy-done.3
  10.7 0.0 copy-done.5
  10.7 0.5 %join.1 = (f32[8,2048]{1,0:T(8,128)S(1)}, f32[8,2048]{1,0:T(8,128)S(1)}) custom-call(f32[8,1536]{1,0:T(8,128)S(1)} %get-tuple-element.15.side, f32[8,512]{1,0:T(8,128)S(1)} %get-tuple-element.16.column, f32[16,1024]{1,0:T(8,128)S(1)} %collective-permute-done.left, f32[16,1024]{1,0:T(8,128)S(1)} %collective-permute-done.1.right, ...), custom_call_target="tpu_custom_call" | custom-call | tf_op jit(solution)/shard_map/join/pallas_call | solution.py:624
  11.2 4.7 %collective-permute-start.2 = (f32[8,2048]{1,0:T(8,128)S(1)}, f32[8,2048]{1,0:T(8,128)S(1)}, u32[]{:S(2)}, u32[]{:S(2)}) collective-permute-start(f32[8,2048]{1,0:T(8,128)S(1)} %get-tuple-element.19), channel_id=1, source_target_pairs={{0,1},{1,2},{2,3},{3,4},{4,5},{5,6},{6,7},{7,8},{8,9},{9,10},{10,1... | collective-permute-start | bytes 196616 | tf_op jit(solution)/shard_map/ppermute | solution.py:220
  15.8 0.0 collective-permute-start.3
  15.8 0.0 copy-done
  15.8 0.0 copy-start.2
  15.8 0.0 copy-start.4
  15.9 5.7 %middle.1 = (f32[8,512,256]{2,1,0:T(8,128)}, f32[4,2,512,128]{3,2,1,0:T(8,128)S(1)}, f32[4,512,128]{2,1,0:T(8,128)S(1)}) custom-call(f32[4,272,256]{2,1,0:T(8,128)S(1)} %get-tuple-element.21.c_own, f32[8,512,256]{2,1,0:T(8,128)} %block.3, f32[16,1024]{1,0:T(8,128)S(1)} %collective-permute-done.left, f32[16,1024]{1,0:T(8,128)S(1)} %collective-permute-done.1.right, ...), custom_call_target="tpu_custom_call" | custom-call | tf_op jit(solution)/shard_map/middle/pallas_call | solution.py:637
  21.6 0.0 collective-permute-done.2.left
  21.6 2.2 %collective-permute-done.3.right = f32[8,2048]{1,0:T(8,128)S(1)} collective-permute-done((f32[8,2048]{1,0:T(8,128)S(1)}, f32[8,2048]{1,0:T(8,128)S(1)}, u32[]{:S(2)}, u32[]{:S(2)}) %collective-permute-start.3) | collective-permute-done | bytes 65568 | tf_op jit(solution)/shard_map/ppermute | solution.py:219
  23.8 0.0 copy-done.2
  23.8 0.0 copy-done.4
  23.8 2.7 %last.1 = f32[8,512,256]{2,1,0:T(8,128)} custom-call(f32[8,2048]{1,0:T(8,128)S(1)} %collective-permute-done.2.left, f32[8,2048]{1,0:T(8,128)S(1)} %collective-permute-done.3.right, bf16[1152,256]{1,0:T(8,128)(2,1)S(1)} %copy-done.2, bf16[3,48,256]{2,1,0:T(8,128)(2,1)S(1)} %copy-done.4, ...), custom_call_target="tpu_custom_call", output_to_operand_aliasing={{}: (6, {})} | custom-call | tf_op jit(solution)/shard_map/last/pallas_call | solution.py:655
Async XLA Ops:
  0.0 6.0 %copy-start.1 = (bf16[3136,256]{1,0:T(8,128)(2,1)S(1)}, bf16[3136,256]{1,0:T(8,128)(2,1)}, u32[]{:S(2)}) copy-start(bf16[3136,256]{1,0:T(8,128)(2,1)} %constant.12.clone.table) | copy-start | bytes 4816900
  1.7 9.0 %collective-permute-start = (f32[16,1024]{1,0:T(8,128)S(1)}, f32[16,1024]{1,0:T(8,128)S(1)}, u32[]{:S(2)}, u32[]{:S(2)}) collective-permute-start(f32[16,1024]{1,0:T(8,128)S(1)} %get-tuple-element.17), channel_id=1, source_target_pairs={{0,32},{32,64},{64,96},{96,128},{128,160},{160,192},{192,224},{224... | collective-permute-start | bytes 196616 | tf_op jit(solution)/shard_map/ppermute | solution.py:220
  3.4 7.3 %copy-start.3 = (bf16[384,384]{1,0:T(8,128)(2,1)S(1)}, bf16[384,384]{1,0:T(8,128)(2,1)}, u32[]{:S(2)}) copy-start(bf16[384,384]{1,0:T(8,128)(2,1)} %constant.14.clone.receive) | copy-start | bytes 884740
  3.4 7.3 %copy-start.5 = (bf16[16,1536]{1,0:T(8,128)(2,1)S(1)}, bf16[16,1536]{1,0:T(8,128)(2,1)}, u32[]{:S(2)}) copy-start(bf16[16,1536]{1,0:T(8,128)(2,1)} %constant.13.clone.y_sent) | copy-start | bytes 147460
  3.4 12.5 %copy-start = (bf16[4368,256]{1,0:T(8,128)(2,1)S(1)}, bf16[4368,256]{1,0:T(8,128)(2,1)}, u32[]{:S(2)}) copy-start(bf16[4368,256]{1,0:T(8,128)(2,1)} %constant.15.clone.table) | copy-start | bytes 6709252
  3.4 7.3 %collective-permute-start.1 = (f32[16,1024]{1,0:T(8,128)S(1)}, f32[16,1024]{1,0:T(8,128)S(1)}, u32[]{:S(2)}, u32[]{:S(2)}) collective-permute-start(f32[16,1024]{1,0:T(8,128)S(1)} %get-tuple-element.18), channel_id=1, source_target_pairs={{32,0},{64,32},{96,64},{128,96},{160,128},{192,160},{224,192},{0,2... | collective-permute-start | bytes 196616 | tf_op jit(solution)/shard_map/ppermute | solution.py:219
  11.2 10.4 %collective-permute-start.2 = (f32[8,2048]{1,0:T(8,128)S(1)}, f32[8,2048]{1,0:T(8,128)S(1)}, u32[]{:S(2)}, u32[]{:S(2)}) collective-permute-start(f32[8,2048]{1,0:T(8,128)S(1)} %get-tuple-element.19), channel_id=1, source_target_pairs={{0,1},{1,2},{2,3},{3,4},{4,5},{5,6},{6,7},{7,8},{8,9},{9,10},{10,1... | collective-permute-start | bytes 196616 | tf_op jit(solution)/shard_map/ppermute | solution.py:220
  15.8 7.9 %collective-permute-start.3 = (f32[8,2048]{1,0:T(8,128)S(1)}, f32[8,2048]{1,0:T(8,128)S(1)}, u32[]{:S(2)}, u32[]{:S(2)}) collective-permute-start(f32[8,2048]{1,0:T(8,128)S(1)} %get-tuple-element.20), channel_id=1, source_target_pairs={{1,0},{2,1},{3,2},{4,3},{5,4},{6,5},{7,6},{8,7},{9,8},{10,9},{11,1... | collective-permute-start | bytes 196616 | tf_op jit(solution)/shard_map/ppermute | solution.py:219
  15.8 7.9 %copy-start.2 = (bf16[1152,256]{1,0:T(8,128)(2,1)S(1)}, bf16[1152,256]{1,0:T(8,128)(2,1)}, u32[]{:S(2)}) copy-start(bf16[1152,256]{1,0:T(8,128)(2,1)} %constant.16.clone.x_level2) | copy-start | bytes 1769476
  15.8 7.9 %copy-start.4 = (bf16[3,48,256]{2,1,0:T(8,128)(2,1)S(1)}, bf16[3,48,256]{2,1,0:T(8,128)(2,1)}, u32[]{:S(2)}) copy-start(bf16[3,48,256]{2,1,0:T(8,128)(2,1)} %constant.17.clone.updates) | copy-start | bytes 221188

commit v2 on v1

--- a/solution.py
+++ b/solution.py
@@ -299,40 +299,40 @@
     to_right[...] = message(1)
 
 
-def own_kernel(z_a, z_d, reach, places, block, table, c, side, column, u, arrived):
+def own_kernel(z_a, z_d, reach, parts, places, block, table, c, side, column, u, arrived):
     planes, halves, fine, lanes = u.shape
-    part = fine // 2
+    size = fine // parts
     copies = [
         [
             pltpu.make_async_copy(
-                block.at[:, pl.ds(at * part, part), pl.ds(h * lanes, lanes)],
-                u.at[:, h, pl.ds(at * part, part), :],
+                block.at[:, pl.ds(at * size, size), pl.ds(h * lanes, lanes)],
+                u.at[:, h, pl.ds(at * size, size), :],
                 arrived.at[at, h],
             )
             for h in range(halves)
         ]
-        for at in range(2)
+        for at in range(parts)
     ]
     for some in copies:
         for copy in some:
             copy.start()
     n, rows, stride = fine // 2, c.shape[1], side.shape[1] // c.shape[0]
-    join = lambda parts: jnp.concatenate(parts, 1)
+    join = lambda pieces_of: jnp.concatenate(pieces_of, 1)
     tables = [unpack(table, place) for place in places]
-    y_table = tables[4]
-    even, x_parts = [], []
-    for at in range(2):
+    y_table = tables[-1]
+    even, found = [], []
+    for at in range(parts):
         for copy in copies[at]:
             copy.wait()
         whole = [
-            join([u[k, h, at * part:(at + 1) * part, :] for h in range(halves)])
+            join([u[k, h, at * size:(at + 1) * size, :] for h in range(halves)])
             for k in range(planes)
         ]
         even.append([
-            join([u[k, h, pl.ds(at * part, part // 2, stride=2), :] for h in range(halves)])
+            join([u[k, h, pl.ds(at * size, size // 2, stride=2), :] for h in range(halves)])
             for k in range(0, planes, 2)
         ])
-        x_parts.append([
+        found.append([
             [
                 dot(tables[2 * at], cut(combine(z_a[z], whole), 0)),
                 dot(tables[2 * at + 1], cut(combine(z_d[z], even[at]), 0)),
@@ -340,18 +340,29 @@
             for z in range(planes // 2)
         ])
 
-    def whole_rows(low, high):
-        middle, edge = n // 2 - reach, n // 2 + reach
-        return jnp.concatenate([
-            low[:middle], low[middle:edge] + high[:2 * reach], high[2 * reach:edge],
-            low[edge:] + high[edge:],
-        ], 0)
+    def whole_rows(values):
+        own, out, tail = size // 2, [], None
+        for at, value in enumerate(values):
+            last = at == parts - 1
+            before = 0 if at == 0 else 2 * reach
+            inside = own - reach * ((at > 0) + (not last))
+            if at:
+                out.append(out.pop() + value[:before])
+            out.append(value[before:before + inside])
+            if not last:
+                out.append(value[before + inside:before + inside + 2 * reach])
+            if at == 0 or last:
+                rest = value[value.shape[0] - (rows - n):]
+                tail = rest if tail is None else tail + rest
+        return jnp.concatenate(out + [tail], 0)
 
     for z in range(planes // 2):
-        x_a = whole_rows(x_parts[0][z][0], x_parts[1][z][0])
-        x_d = whole_rows(x_parts[0][z][1], x_parts[1][z][1])
+        x_a = whole_rows([some[z][0] for some in found])
+        x_d = whole_rows([some[z][1] for some in found])
         odd_lane = iota(x_d.shape, 1) % 2 == 1
-        field = jnp.concatenate([even[0][z], even[1][z], jnp.zeros((rows - n, halves * lanes), F32)], 0)
+        field = jnp.concatenate(
+            [some[z] for some in even] + [jnp.zeros((rows - n, halves * lanes), F32)], 0
+        )
         x_de = jnp.where(odd_lane, pltpu.roll(field, 1, 1), x_d)
         total = dot(join([cut(x_a, 1), cut(x_de, 1)]), y_table)
         total = total + jnp.where(odd_lane, 0.0, field)
@@ -408,13 +419,22 @@
 def middle_kernel(
     z_a, z_d, places, c_own, block, left, right, table, out, w, edge, u, inner, ready, arrived, sent
 ):
-    planes, halves, fine, lanes = u.shape
+    planes, halves, fine, lanes = u.shape[0], u.shape[1], block.shape[1], u.shape[3]
+    cuts = (0, fine // 2 + 8, fine)
     copies = [
-        pltpu.make_async_copy(block.at[:, :, pl.ds(h * lanes, lanes)], u.at[:, h], arrived.at[h])
-        for h in range(halves)
+        [
+            pltpu.make_async_copy(
+                block.at[:, pl.ds(start, stop - start), pl.ds(h * lanes, lanes)],
+                u.at[:, h, pl.ds(start, stop - start), :],
+                arrived.at[turn, h],
+            )
+            for h in range(halves)
+        ]
+        for turn, (start, stop) in enumerate(zip(cuts, cuts[1:]))
     ]
-    for copy in copies:
-        copy.start()
+    for some in copies:
+        for copy in some:
+            copy.start()
     half, rows, width = c_own.shape
     n, quarter = fine // 2, fine // 4
     from_left, from_right = left[...], right[...]
@@ -449,48 +469,62 @@
                 here = (z, h, pl.ds(0, quarter, stride=2), slice(None))
                 inner[here] = inner[here] + added[:, h * lanes:(h + 1) * lanes]
 
-    for copy in copies:
-        copy.wait()
-    last_row = iota((n, width), 0) == n - 1
-    even_lane = iota((n, width), 1) % 2 == 0
-
-    def rows_of(k):
-        load = lambda start: jnp.concatenate(
-            [u[k, h, pl.ds(start, n, stride=2), :] for h in range(halves)], 1
-        )
-        even, odd = load(0), load(1)
-        at = (k // 2) * width
-        halo = from_right[10 + k % 2:11 + k % 2, at:at + width]
-        after = jnp.where(last_row, halo, pltpu.roll(even, n - 1, 0))
-        return even, odd - 0.5 * (even + after)
+    for k in range(planes):
+        for h in range(halves):
+            at = (k // 2) * width + h * lanes
+            u[k, h, fine:fine + 1, :] = from_right[10 + k % 2:11 + k % 2, at:at + lanes]
+    size = 32
+    lane = iota((size, width), 1)
+    odd_lane, last_lane = lane % 2 == 1, lane == width - 1
 
     def along_y(part):
-        after = jnp.where(iota(part.shape, 1) == width - 1, 0.0, pltpu.roll(part, width - 1, 1))
-        return jnp.where(even_lane, part, part - 0.5 * (pltpu.roll(part, 1, 1) + after))
-
-    def store(k, start, part):
-        for h in range(halves):
-            target = w.at[k // 2, h] if k % 2 == 0 else (
-                edge.at[k // 2] if h == halves - 1 else ready.at[k // 2, h])
-            target[pl.ds(start, n, stride=2), :] = part[:, h * lanes:(h + 1) * lanes]
-
-    begin = rows_of(0)
-    here, done = begin, []
-    for k in range(0, planes, 2):
-        held = jnp.concatenate([inner[k // 2, h] for h in range(halves)], 1)
-        store(k, 0, jnp.where(even_lane, held, along_y(here[0])))
-        store(k, 1, along_y(here[1]))
-        following = begin if k + 2 == planes else rows_of(k + 2)
-        between = rows_of(k + 1)
-        for start in (0, 1):
-            store(k + 1, start, along_y(between[start] - 0.5 * (here[start] + following[start])))
-        for h in range(halves - 1):
-            copy = pltpu.make_async_copy(
-                ready.at[k // 2, h], out.at[k + 1, :, pl.ds(h * lanes, lanes)], sent.at[k // 2, h]
+        after = jnp.where(last_lane, 0.0, pltpu.roll(part, width - 1, 1))
+        return jnp.where(odd_lane, part - 0.5 * (pltpu.roll(part, 1, 1) + after), part)
+
+    def some_rows(step, carry):
+        start, spot = step * 2 * size, step * size
+
+        def rows_of(k):
+            load = lambda first: jnp.concatenate(
+                [u[k, h, pl.ds(first, size, stride=2), :] for h in range(halves)], 1
             )
-            copy.start()
-            done.append(copy)
-        here = following
+            even = load(start)
+            return even, load(start + 1) - 0.5 * (even + load(start + 2))
+
+        def store(k, odd, part):
+            for h in range(halves):
+                target = w.at[k // 2, h] if k % 2 == 0 else (
+                    edge.at[k // 2] if h == halves - 1 else ready.at[k // 2, h])
+                target[pl.ds(start + odd, size, stride=2), :] = part[:, h * lanes:(h + 1) * lanes]
+
+        begin = rows_of(0)
+        here = begin
+        for k in range(0, planes, 2):
+            held = jnp.concatenate([inner[k // 2, h, pl.ds(spot, size), :] for h in range(halves)], 1)
+            store(k, 0, jnp.where(odd_lane, along_y(here[0]), held))
+            store(k, 1, along_y(here[1]))
+            following = begin if k + 2 == planes else rows_of(k + 2)
+            between = rows_of(k + 1)
+            for odd in (0, 1):
+                store(k + 1, odd, along_y(between[odd] - 0.5 * (here[odd] + following[odd])))
+            here = following
+        return carry
+
+    done, steps = [], n // size
+    for turn in range(2):
+        for copy in copies[turn]:
+            copy.wait()
+        for step in range(turn * steps // 2, (turn + 1) * steps // 2):
+            some_rows(step, 0)
+        here = pl.ds(turn * n, n)
+        for z in range(half):
+            for h in range(halves - 1):
+                done.append(pltpu.make_async_copy(
+                    ready.at[z, h, here, :],
+                    out.at[2 * z + 1, here, pl.ds(h * lanes, lanes)],
+                    sent.at[turn, z, h],
+                ))
+                done[-1].start()
     for copy in done:
         copy.wait()
 
@@ -596,26 +630,24 @@
     )(density)
     left_x, right_x = exchange(to_left, to_right, "gx")
 
-    reach = min(16, n // 2)
-    tail = list(range(n, rows))
-    front = list(range(n // 2 + reach)) + tail
-    back = list(range(n // 2 - reach, n)) + tail
-    packed, places = pack(
-        [
-            pieces(own_a[front][:, :n], 1), pieces(own_d[front][:, :n // 2], 1),
-            pieces(own_a[back][:, n:], 1), pieces(own_d[back][:, n // 2:], 1),
-            y_table,
-        ],
-        width,
-    )
+    reach, parts = 16, 4
+    size = n // parts
+    own_tables = []
+    for at in range(parts):
+        near = list(range(max(0, at * size - reach), min(n, (at + 1) * size + reach)))
+        if at in (0, parts - 1):
+            near += list(range(n, rows))
+        fine_at, even_at = slice(2 * at * size, 2 * (at + 1) * size), slice(at * size, (at + 1) * size)
+        own_tables += [pieces(own_a[near][:, fine_at], 1), pieces(own_d[near][:, even_at], 1)]
+    packed, places = pack(own_tables + [y_table], width)
     c_own, side, column = pl.pallas_call(
-        functools.partial(own_kernel, z_a, z_d, reach, places),
+        functools.partial(own_kernel, z_a, z_d, reach, parts, places),
         out_shape=(shape(half, rows, width), shape(8, half * stride), shape(planes, fine)),
         in_specs=[hbm, vmem],
         out_specs=[vmem] * 3,
         scratch_shapes=[
             pltpu.VMEM((planes, halves, fine, lanes), F32),
-            pltpu.SemaphoreType.DMA((2, halves)),
+            pltpu.SemaphoreType.DMA((parts, halves)),
         ],
         compiler_params=params(50),
         name="own",
@@ -642,11 +674,11 @@
         in_specs=[vmem, hbm, vmem, vmem, vmem],
         out_specs=[hbm, vmem, vmem],
         scratch_shapes=[
-            pltpu.VMEM((planes, halves, fine, lanes), F32),
+            pltpu.VMEM((planes, halves, fine + 8, lanes), F32),
             pltpu.VMEM((half, halves, n, lanes), F32),
             pltpu.VMEM((half, halves - 1, fine, lanes), F32),
-            pltpu.SemaphoreType.DMA((halves,)),
-            pltpu.SemaphoreType.DMA((half, halves - 1)),
+            pltpu.SemaphoreType.DMA((2, halves)),
+            pltpu.SemaphoreType.DMA((2, half, halves - 1)),
         ],
         compiler_params=params(44),
         name="middle",

time: 26.5 us -> 26.3 us (level)
  Pallas kernels: 15.2 us -> 14.2 us
  waiting for transfers between devices: 2.16 us -> 2.97 us
    pallas_call x1, Pallas kernels: 5.72 us -> 4.92 us  [shards(): pl.pallas_call(functools.partial(middle_kernel, z2_a, z2_d, places), out_...]
    ppermute x2, waiting for transfers between devices: 2.16 us -> 2.96 us  [exchange(): right = lax.ppermute(to_left, axis, backward)]
  transfers between devices with their start and end apart: 4 -> 4, of which waited for: 1 -> 1; matrix products, arithmetic and copies ran while one was open for 0% -> 0% of each run, Pallas kernels for 39% -> 36%
where the time goes in v2:
time: 26.3 us; the launch traced here: 26.2 us
  Pallas kernels  14.2 us (54%)
  starting transfers between devices  8.97 us (34%)
  waiting for transfers between devices  2.97 us (11%)
    ppermute x2, starting transfers between devices, exchange(): return (lax.ppermute(to_right, axis, forward), right)  6.39 us
    pallas_call x1, Pallas kernels, shards(): pl.pallas_call(functools.partial(middle_kernel, z2_a, z2_d, places), out_...  4.92 us
    pallas_call x1, Pallas kernels, shards(): pl.pallas_call(functools.partial(own_kernel, z_a, z_d, reach, parts, plac...  4.49 us
    ppermute x2, waiting for transfers between devices, exchange(): right = lax.ppermute(to_left, axis, backward)  2.96 us
    pallas_call x1, Pallas kernels, shards(): pl.pallas_call(functools.partial(last_kernel, z2_a, z2_d), out_shape=shap...  2.66 us
    ppermute x2, starting transfers between devices, exchange(): right = lax.ppermute(to_left, axis, backward)  2.57 us
    pallas_call x1, Pallas kernels, shards(): pl.pallas_call(functools.partial(edge_kernel, (send[0][:, :depth], send[1...  1.65 us
  transfers between devices with their start and end apart: 4, of which 1 were waited for; matrix products, arithmetic and copies ran while one was open for 0% of the time, Pallas kernels for 36%

profile of v2, /device:TPU:71, one launch (start us, length us, event | category | flops | bytes accessed | tf_op | source)
XLA Modules:
  0.0 26.2 jit_solution(8178411289629632226)
XLA Ops:
  0.0 0.0 copy-start.1
  0.0 1.6 %edges.1 = (f32[16,1024]{1,0:T(8,128)S(1)}, f32[16,1024]{1,0:T(8,128)S(1)}) custom-call(f32[8,512,256]{2,1,0:T(8,128)} %block.3), custom_call_target="tpu_custom_call" | custom-call | tf_op jit(solution)/shard_map/edges/pallas_call | solution.py:619
  1.7 1.7 %collective-permute-start = (f32[16,1024]{1,0:T(8,128)S(1)}, f32[16,1024]{1,0:T(8,128)S(1)}, u32[]{:S(2)}, u32[]{:S(2)}) collective-permute-start(f32[16,1024]{1,0:T(8,128)S(1)} %get-tuple-element.17), channel_id=1, source_target_pairs={{0,32},{32,64},{64,96},{96,128},{128,160},{160,192},{192,224},{224... | collective-permute-start | bytes 196616 | tf_op jit(solution)/shard_map/ppermute | solution.py:220
  3.4 0.0 copy-start.3
  3.4 0.0 copy-start.5
  3.4 0.0 copy-start
  3.4 2.6 %collective-permute-start.1 = (f32[16,1024]{1,0:T(8,128)S(1)}, f32[16,1024]{1,0:T(8,128)S(1)}, u32[]{:S(2)}, u32[]{:S(2)}) collective-permute-start(f32[16,1024]{1,0:T(8,128)S(1)} %get-tuple-element.18), channel_id=1, source_target_pairs={{32,0},{64,32},{96,64},{128,96},{160,128},{192,160},{224,192},{0,2... | collective-permute-start | bytes 196616 | tf_op jit(solution)/shard_map/ppermute | solution.py:219
  6.0 0.0 copy-done.1
  6.0 4.5 %own.1 = (f32[4,272,256]{2,1,0:T(8,128)S(1)}, f32[8,1536]{1,0:T(8,128)S(1)}, f32[8,512]{1,0:T(8,128)S(1)}) custom-call(f32[8,512,256]{2,1,0:T(8,128)} %block.3, bf16[2688,256]{1,0:T(8,128)(2,1)S(1)} %copy-done.1), custom_call_target="tpu_custom_call" | custom-call | tf_op jit(solution)/shard_map/own/pallas_call | solution.py:643
  10.5 0.0 collective-permute-done.left
  10.5 0.0 collective-permute-done.1.right
  10.5 0.0 copy-done.3
  10.5 0.0 copy-done.5
  10.5 0.5 %join.1 = (f32[8,2048]{1,0:T(8,128)S(1)}, f32[8,2048]{1,0:T(8,128)S(1)}) custom-call(f32[8,1536]{1,0:T(8,128)S(1)} %get-tuple-element.15.side, f32[8,512]{1,0:T(8,128)S(1)} %get-tuple-element.16.column, f32[16,1024]{1,0:T(8,128)S(1)} %collective-permute-done.left, f32[16,1024]{1,0:T(8,128)S(1)} %collective-permute-done.1.right, ...), custom_call_target="tpu_custom_call" | custom-call | tf_op jit(solution)/shard_map/join/pallas_call | solution.py:656
  11.0 4.7 %collective-permute-start.2 = (f32[8,2048]{1,0:T(8,128)S(1)}, f32[8,2048]{1,0:T(8,128)S(1)}, u32[]{:S(2)}, u32[]{:S(2)}) collective-permute-start(f32[8,2048]{1,0:T(8,128)S(1)} %get-tuple-element.19), channel_id=1, source_target_pairs={{0,1},{1,2},{2,3},{3,4},{4,5},{5,6},{6,7},{7,8},{8,9},{9,10},{10,1... | collective-permute-start | bytes 196616 | tf_op jit(solution)/shard_map/ppermute | solution.py:220
  15.6 0.0 collective-permute-start.3
  15.6 0.0 copy-done
  15.6 0.0 copy-start.2
  15.6 0.0 copy-start.4
  15.6 4.9 %middle.1 = (f32[8,512,256]{2,1,0:T(8,128)}, f32[4,2,512,128]{3,2,1,0:T(8,128)S(1)}, f32[4,512,128]{2,1,0:T(8,128)S(1)}) custom-call(f32[4,272,256]{2,1,0:T(8,128)S(1)} %get-tuple-element.21.c_own, f32[8,512,256]{2,1,0:T(8,128)} %block.3, f32[16,1024]{1,0:T(8,128)S(1)} %collective-permute-done.left, f32[16,1024]{1,0:T(8,128)S(1)} %collective-permute-done.1.right, ...), custom_call_target="tpu_custom_call" | custom-call | tf_op jit(solution)/shard_map/middle/pallas_call | solution.py:669
  20.6 0.0 collective-permute-done.2.left
  20.6 3.0 %collective-permute-done.3.right = f32[8,2048]{1,0:T(8,128)S(1)} collective-permute-done((f32[8,2048]{1,0:T(8,128)S(1)}, f32[8,2048]{1,0:T(8,128)S(1)}, u32[]{:S(2)}, u32[]{:S(2)}) %collective-permute-start.3) | collective-permute-done | bytes 65568 | tf_op jit(solution)/shard_map/ppermute | solution.py:219
  23.5 0.0 copy-done.2
  23.5 0.0 copy-done.4
  23.5 2.7 %last.1 = f32[8,512,256]{2,1,0:T(8,128)} custom-call(f32[8,2048]{1,0:T(8,128)S(1)} %collective-permute-done.2.left, f32[8,2048]{1,0:T(8,128)S(1)} %collective-permute-done.3.right, bf16[1152,256]{1,0:T(8,128)(2,1)S(1)} %copy-done.2, bf16[3,48,256]{2,1,0:T(8,128)(2,1)S(1)} %copy-done.4, ...), custom_call_target="tpu_custom_call", output_to_operand_aliasing={{}: (6, {})} | custom-call | tf_op jit(solution)/shard_map/last/pallas_call | solution.py:687
Async XLA Ops:
  0.0 6.0 %copy-start.1 = (bf16[2688,256]{1,0:T(8,128)(2,1)S(1)}, bf16[2688,256]{1,0:T(8,128)(2,1)}, u32[]{:S(2)}) copy-start(bf16[2688,256]{1,0:T(8,128)(2,1)} %constant.12.clone.table) | copy-start | bytes 4128772
  1.7 8.8 %collective-permute-start = (f32[16,1024]{1,0:T(8,128)S(1)}, f32[16,1024]{1,0:T(8,128)S(1)}, u32[]{:S(2)}, u32[]{:S(2)}) collective-permute-start(f32[16,1024]{1,0:T(8,128)S(1)} %get-tuple-element.17), channel_id=1, source_target_pairs={{0,32},{32,64},{64,96},{96,128},{128,160},{160,192},{192,224},{224... | collective-permute-start | bytes 196616 | tf_op jit(solution)/shard_map/ppermute | solution.py:220
  3.4 7.1 %copy-start.3 = (bf16[384,384]{1,0:T(8,128)(2,1)S(1)}, bf16[384,384]{1,0:T(8,128)(2,1)}, u32[]{:S(2)}) copy-start(bf16[384,384]{1,0:T(8,128)(2,1)} %constant.14.clone.receive) | copy-start | bytes 884740
  3.4 7.1 %copy-start.5 = (bf16[16,1536]{1,0:T(8,128)(2,1)S(1)}, bf16[16,1536]{1,0:T(8,128)(2,1)}, u32[]{:S(2)}) copy-start(bf16[16,1536]{1,0:T(8,128)(2,1)} %constant.13.clone.y_sent) | copy-start | bytes 147460
  3.4 12.3 %copy-start = (bf16[4368,256]{1,0:T(8,128)(2,1)S(1)}, bf16[4368,256]{1,0:T(8,128)(2,1)}, u32[]{:S(2)}) copy-start(bf16[4368,256]{1,0:T(8,128)(2,1)} %constant.15.clone.table) | copy-start | bytes 6709252
  3.4 7.1 %collective-permute-start.1 = (f32[16,1024]{1,0:T(8,128)S(1)}, f32[16,1024]{1,0:T(8,128)S(1)}, u32[]{:S(2)}, u32[]{:S(2)}) collective-permute-start(f32[16,1024]{1,0:T(8,128)S(1)} %get-tuple-element.18), channel_id=1, source_target_pairs={{32,0},{64,32},{96,64},{128,96},{160,128},{192,160},{224,192},{0,2... | collective-permute-start | bytes 196616 | tf_op jit(solution)/shard_map/ppermute | solution.py:219
  11.0 9.6 %collective-permute-start.2 = (f32[8,2048]{1,0:T(8,128)S(1)}, f32[8,2048]{1,0:T(8,128)S(1)}, u32[]{:S(2)}, u32[]{:S(2)}) collective-permute-start(f32[8,2048]{1,0:T(8,128)S(1)} %get-tuple-element.19), channel_id=1, source_target_pairs={{0,1},{1,2},{2,3},{3,4},{4,5},{5,6},{6,7},{7,8},{8,9},{9,10},{10,1... | collective-permute-start | bytes 196616 | tf_op jit(solution)/shard_map/ppermute | solution.py:220
  15.6 7.9 %collective-permute-start.3 = (f32[8,2048]{1,0:T(8,128)S(1)}, f32[8,2048]{1,0:T(8,128)S(1)}, u32[]{:S(2)}, u32[]{:S(2)}) collective-permute-start(f32[8,2048]{1,0:T(8,128)S(1)} %get-tuple-element.20), channel_id=1, source_target_pairs={{1,0},{2,1},{3,2},{4,3},{5,4},{6,5},{7,6},{8,7},{9,8},{10,9},{11,1... | collective-permute-start | bytes 196616 | tf_op jit(solution)/shard_map/ppermute | solution.py:219
  15.6 7.9 %copy-start.2 = (bf16[1152,256]{1,0:T(8,128)(2,1)S(1)}, bf16[1152,256]{1,0:T(8,128)(2,1)}, u32[]{:S(2)}) copy-start(bf16[1152,256]{1,0:T(8,128)(2,1)} %constant.16.clone.x_level2) | copy-start | bytes 1769476
  15.6 7.9 %copy-start.4 = (bf16[3,48,256]{2,1,0:T(8,128)(2,1)S(1)}, bf16[3,48,256]{2,1,0:T(8,128)(2,1)}, u32[]{:S(2)}) copy-start(bf16[3,48,256]{2,1,0:T(8,128)(2,1)} %constant.17.clone.updates) | copy-start | bytes 221188
